TPU v7x, 32 devices: a whole 2x2x4 slice. The times are simulated.
32 devices in a mesh: clips: 2 (over x), rows: 16 (over z, y, core).
Axes of the slice: x: 2, y: 2, z: 4, core: 2. Of those that a mesh axis runs over, the one named last changes fastest.
Arguments:
- latents: bfloat16 [8, 64, 160, 384], P('clips', 'rows'), parts along dimension 0, may hold values from -6 to 6
- gamma: float32 [384], replicated, may hold values from 0.5 to 1.5
- weight: bfloat16 [3, 3, 3, 384, 384], replicated, may hold values from -0.0625 to 0.0625
- bias: float32 [384], replicated, may hold values from -3 to 3
- intersection: int32 [32], P('clips'), parts along dimension 0, may hold values from 0 to 2
- ramp: int32 [32], P('clips'), parts along dimension 0, may hold values from 1 to 3
Outputs:
- decoded: bfloat16 [8, 64, 160, 384], P('clips', 'rows'), parts along dimension 0
There are 2 independent parts, one for each index of `clips`. A program takes and returns all parts, laid end to end along the dimension named above; an argument that names none is the same for every part. Nothing has to cross between parts.
All inputs are finite; a program needn't handle non-finite values.
Results may differ from a plain program's by a relative error of at most 0.0034.
Values may be sent and summed in bfloat16 or wider, within the bound.
No kernel may reach another device: no remote copies, remote signals or barrier semaphores. Data moves between devices by JAX's collectives and lax.ppermute only.
A program may use at most 448 MiB of HBM per device.

v0:
```python
import jax
import jax.numpy as jnp
from jax import lax
from jax.sharding import PartitionSpec as P

OV_MAX = 2


def shifted(block, axis, distance):
    devices = range(lax.axis_size(axis))
    route = [(i - distance, i) for i in devices if i - distance in devices]
    return lax.ppermute(block, axis, route)


def activate(tile, gamma, keep):
    values = tile.astype(jnp.float32)
    square = jnp.mean(values * values, axis=-1, keepdims=True)
    normed = values * lax.rsqrt(square + 1e-06) * gamma
    return (jax.nn.silu(normed) * keep).astype(jnp.bfloat16)


def convolve(stacked, weight, bias, count):
    padded = jnp.pad(stacked, ((0, 0), (1, 1), (1, 1), (0, 0)))
    height = stacked.shape[1]
    width = stacked.shape[2]
    total = jnp.zeros((count, height, width, weight.shape[4]), jnp.float32)
    for step_t in range(3):
        for step_h in range(3):
            for step_w in range(3):
                slab = padded[
                    step_t : step_t + count, step_h : step_h + height, step_w : step_w + width
                ]
                total = total + jnp.einsum(
                    "fhwc,cd->fhwd",
                    slab,
                    weight[step_t, step_h, step_w],
                    preferred_element_type=jnp.float32,
                )
    return total + bias


def per_device(latents, gamma, weight, bias, intersection, ramp):
    frames = latents.shape[0]
    rows = latents.shape[1]
    extra = OV_MAX
    index = lax.axis_index("rows")
    count = lax.axis_size("rows")
    own_ov = jnp.where(index == count - 1, 0, intersection[index])
    previous = jnp.maximum(index - 1, 0)
    prev_ov = jnp.where(index > 0, intersection[previous], 0)
    prev_ramp = ramp[previous]
    places = jnp.arange(rows + extra, dtype=jnp.int32)
    keep = (places < rows + own_ov).astype(jnp.float32).reshape(1, -1, 1, 1)
    offsets = jnp.arange(extra, dtype=jnp.int32)
    blend_w = jnp.where(
        offsets < prev_ov,
        jnp.maximum(prev_ramp - offsets, 0).astype(jnp.float32)
        / (prev_ramp + 1).astype(jnp.float32),
        jnp.float32(0.0),
    )
    blend_w = blend_w.reshape(1, -1, 1, 1)
    width = latents.shape[2]
    chans = latents.shape[3]
    below = shifted(latents, "rows", -1)
    tile = jnp.concatenate([latents, below[:, :extra]], axis=1)
    start = jnp.zeros((2, rows + extra, width, chans), jnp.bfloat16)
    act = activate(tile, gamma, keep)
    stacked = jnp.concatenate([start, act], axis=0)
    outcome = (tile.astype(jnp.float32) + convolve(stacked, weight, bias, frames)).astype(
        jnp.bfloat16
    )
    outcome, unused = (outcome, stacked[frames:])
    arrived = shifted(outcome[:, rows:], "rows", 1)
    own_rows = outcome[:, :rows]
    head = own_rows[:, :extra].astype(jnp.float32)
    mixed = blend_w * arrived.astype(jnp.float32) + (1.0 - blend_w) * head
    return jnp.concatenate([mixed.astype(jnp.bfloat16), own_rows[:, extra:]], axis=1)


def solution(mesh):
    in_specs = (P("clips", "rows", None, None), P(), P(), P(), P("clips"), P("clips"))
    out_specs = P("clips", "rows", None, None)
    return jax.shard_map(
        per_device, mesh=mesh, in_specs=in_specs, out_specs=out_specs, check_vma=False
    )
```

profile of v0, /device:TPU:1, one launch (start us, length us, event | category | flops | bytes accessed | tf_op | source)
XLA Modules:
  0.0 218.2 jit_solution(15525754383371504543)
XLA Ops:
  0.0 2.0 collective-permute-start
  2.0 1.3 fusion.116
  4.0 0.0 copy-start
  4.0 0.0 copy-start.2
  4.0 23.0 %collective-permute-done = bf16[4,4,160,384]{3,2,1,0:T(8,128)(2,1)S(1)} collective-permute-done((bf16[4,4,160,384]{3,2,1,0:T(8,128)(2,1)}, bf16[4,4,160,384]{3,2,1,0:T(8,128)(2,1)S(1)}, u32[]{:S(2)}, u32[]{:S(2)}) %collective-permute-start) | collective-permute-done | bytes 1966112 | tf_op jit(solution)/shard_map/ppermute | solution.py:12
  27.0 0.1 slice.235
  27.2 0.0 copy-start.1
  27.2 2.8 %fusion = f32[4,6,160]{2,1,0:T(8,128)S(1)} fusion(bf16[4,2,160,384]{3,2,1,0:T(8,128)(2,1)S(1)} %slice.235, bf16[4,4,160,384]{3,2,1,0:T(8,128)(2,1)} %param.6), kind=kLoop, calls=%fused_computation.27 | loop fusion | flops 5894400 | bytes 2964480 | tf_op jit(solution)/shard_map/reduce_sum | solution.py:17
  30.0 0.0 copy-done
  30.0 4.0 %fusion.8 = bf16[4,6,160,384]{3,2,1,0:T(8,128)(2,1)S(1)} fusion(f32[6]{0:T(128)S(1)} %compare_convert_fusion, f32[384]{0:T(512)} %param.7, f32[4,6,160]{2,1,0:T(8,128)S(1)} %add_rsqrt_fusion, bf16[4,2,160,384]{3,2,1,0:T(8,128)(2,1)S(1)} %slice.235, bf16[4,4,160,384]{3,2,1,0:T(8,128)(2,1)S(1)} %copy-done), kind=kLoop, calls=%fused_computation.35 | loop fusion | flops 14745600 | bytes 5915160 | tf_op jit(solution)/shard_map/convert_element_type | solution.py:19
  34.1 0.0 copy-done.2
  34.1 4.5 %fusion.11 = f32[4,6,160,384]{3,2,1,0:T(8,128)} fusion(bf16[4,6,160,384]{3,2,1,0:T(8,128)(2,1)S(1)} %fusion.8, bf16[3,3,3,384,384]{4,3,2,1,0:T(8,128)(2,1)S(1)} %copy-done.2), kind=kOutput, calls=%fused_computation.38 | convolution fusion | flops 1132462080 | bytes 9142272 | tf_op jit(solution)/shard_map/fhwc,cd->fhwd/dot_general | solution.py:33
  38.6 0.0 copy-done.1
  38.6 4.4 %fusion.12 = f32[4,6,160,384]{3,2,1,0:T(8,128)} fusion(bf16[4,6,160,384]{3,2,1,0:T(8,128)(2,1)S(1)} %fusion.8, bf16[3,3,3,384,384]{4,3,2,1,0:T(8,128)(2,1)S(1)} %copy-done.2), kind=kOutput, calls=%fused_computation.39 | convolution fusion | flops 1132462080 | bytes 9142272 | tf_op jit(solution)/shard_map/fhwc,cd->fhwd/dot_general | solution.py:33
  43.0 4.5 %fusion.13 = f32[4,6,160,384]{3,2,1,0:T(8,128)} fusion(bf16[4,6,160,384]{3,2,1,0:T(8,128)(2,1)S(1)} %fusion.8, bf16[3,3,3,384,384]{4,3,2,1,0:T(8,128)(2,1)S(1)} %copy-done.2), kind=kOutput, calls=%fused_computation.40 | convolution fusion | flops 1132462080 | bytes 9142272 | tf_op jit(solution)/shard_map/fhwc,cd->fhwd/dot_general | solution.py:33
  47.4 4.4 %fusion.14 = f32[4,6,160,384]{3,2,1,0:T(8,128)} fusion(bf16[4,6,160,384]{3,2,1,0:T(8,128)(2,1)S(1)} %fusion.8, bf16[3,3,3,384,384]{4,3,2,1,0:T(8,128)(2,1)S(1)} %copy-done.2), kind=kOutput, calls=%fused_computation.41 | convolution fusion | flops 1132462080 | bytes 9142272 | tf_op jit(solution)/shard_map/fhwc,cd->fhwd/dot_general | solution.py:33
  51.9 4.4 %fusion.15 = f32[4,6,160,384]{3,2,1,0:T(8,128)} fusion(bf16[4,6,160,384]{3,2,1,0:T(8,128)(2,1)S(1)} %fusion.8, bf16[3,3,3,384,384]{4,3,2,1,0:T(8,128)(2,1)S(1)} %copy-done.2), kind=kOutput, calls=%fused_computation.42 | convolution fusion | flops 1132462080 | bytes 9142272 | tf_op jit(solution)/shard_map/fhwc,cd->fhwd/dot_general | solution.py:33
  56.3 4.4 %fusion.16 = f32[4,6,160,384]{3,2,1,0:T(8,128)} fusion(bf16[4,6,160,384]{3,2,1,0:T(8,128)(2,1)S(1)} %fusion.8, bf16[3,3,3,384,384]{4,3,2,1,0:T(8,128)(2,1)S(1)} %copy-done.2), kind=kOutput, calls=%fused_computation.43 | convolution fusion | flops 1132462080 | bytes 9142272 | tf_op jit(solution)/shard_map/fhwc,cd->fhwd/dot_general | solution.py:33
  60.7 4.6 %fusion.17 = f32[4,6,160,384]{3,2,1,0:T(8,128)} fusion(bf16[4,6,160,384]{3,2,1,0:T(8,128)(2,1)S(1)} %fusion.8, bf16[3,3,3,384,384]{4,3,2,1,0:T(8,128)(2,1)S(1)} %copy-done.2), kind=kOutput, calls=%fused_computation.44 | convolution fusion | flops 1132462080 | bytes 9142272 | tf_op jit(solution)/shard_map/fhwc,cd->fhwd/dot_general | solution.py:33
  65.4 4.4 %fusion.18 = f32[4,6,160,384]{3,2,1,0:T(8,128)} fusion(bf16[4,6,160,384]{3,2,1,0:T(8,128)(2,1)S(1)} %fusion.8, bf16[3,3,3,384,384]{4,3,2,1,0:T(8,128)(2,1)S(1)} %copy-done.2), kind=kOutput, calls=%fused_computation.45 | convolution fusion | flops 1132462080 | bytes 9142272 | tf_op jit(solution)/shard_map/fhwc,cd->fhwd/dot_general | solution.py:33
  69.8 4.5 %fusion.19 = f32[4,6,160,384]{3,2,1,0:T(8,128)} fusion(bf16[4,6,160,384]{3,2,1,0:T(8,128)(2,1)S(1)} %fusion.8, bf16[3,3,3,384,384]{4,3,2,1,0:T(8,128)(2,1)S(1)} %copy-done.2), kind=kOutput, calls=%fused_computation.46 | convolution fusion | flops 1132462080 | bytes 9142272 | tf_op jit(solution)/shard_map/fhwc,cd->fhwd/dot_general | solution.py:33
  74.3 4.4 %fusion.20 = f32[4,6,160,384]{3,2,1,0:T(8,128)} fusion(bf16[4,6,160,384]{3,2,1,0:T(8,128)(2,1)S(1)} %fusion.8, bf16[3,3,3,384,384]{4,3,2,1,0:T(8,128)(2,1)S(1)} %copy-done.2), kind=kOutput, calls=%fused_computation.47 | convolution fusion | flops 1132462080 | bytes 9142272 | tf_op jit(solution)/shard_map/fhwc,cd->fhwd/dot_general | solution.py:33
  78.7 4.4 %fusion.21 = f32[4,6,160,384]{3,2,1,0:T(8,128)} fusion(bf16[4,6,160,384]{3,2,1,0:T(8,128)(2,1)S(1)} %fusion.8, bf16[3,3,3,384,384]{4,3,2,1,0:T(8,128)(2,1)S(1)} %copy-done.2), kind=kOutput, calls=%fused_computation.48 | convolution fusion | flops 1132462080 | bytes 9142272 | tf_op jit(solution)/shard_map/fhwc,cd->fhwd/dot_general | solution.py:33
  83.1 4.6 %fusion.22 = f32[4,6,160,384]{3,2,1,0:T(8,128)} fusion(bf16[4,6,160,384]{3,2,1,0:T(8,128)(2,1)S(1)} %fusion.8, bf16[3,3,3,384,384]{4,3,2,1,0:T(8,128)(2,1)S(1)} %copy-done.2), kind=kOutput, calls=%fused_computation.49 | convolution fusion | flops 1132462080 | bytes 9142272 | tf_op jit(solution)/shard_map/fhwc,cd->fhwd/dot_general | solution.py:33
  87.7 4.6 %fusion.23 = f32[4,6,160,384]{3,2,1,0:T(8,128)} fusion(bf16[4,6,160,384]{3,2,1,0:T(8,128)(2,1)S(1)} %fusion.8, bf16[3,3,3,384,384]{4,3,2,1,0:T(8,128)(2,1)S(1)} %copy-done.2), kind=kOutput, calls=%fused_computation.50 | convolution fusion | flops 1132462080 | bytes 9142272 | tf_op jit(solution)/shard_map/fhwc,cd->fhwd/dot_general | solution.py:33
  92.4 4.6 %fusion.24 = f32[4,6,160,384]{3,2,1,0:T(8,128)} fusion(bf16[4,6,160,384]{3,2,1,0:T(8,128)(2,1)S(1)} %fusion.8, bf16[3,3,3,384,384]{4,3,2,1,0:T(8,128)(2,1)S(1)} %copy-done.2), kind=kOutput, calls=%fused_computation.51 | convolution fusion | flops 1132462080 | bytes 9142272 | tf_op jit(solution)/shard_map/fhwc,cd->fhwd/dot_general | solution.py:33
  96.9 4.5 %fusion.25 = f32[4,6,160,384]{3,2,1,0:T(8,128)} fusion(bf16[4,6,160,384]{3,2,1,0:T(8,128)(2,1)S(1)} %fusion.8, bf16[3,3,3,384,384]{4,3,2,1,0:T(8,128)(2,1)S(1)} %copy-done.2), kind=kOutput, calls=%fused_computation.52 | convolution fusion | flops 1132462080 | bytes 9142272 | tf_op jit(solution)/shard_map/fhwc,cd->fhwd/dot_general | solution.py:33
  101.4 4.4 %fusion.26 = f32[4,6,160,384]{3,2,1,0:T(8,128)} fusion(bf16[4,6,160,384]{3,2,1,0:T(8,128)(2,1)S(1)} %fusion.8, bf16[3,3,3,384,384]{4,3,2,1,0:T(8,128)(2,1)S(1)} %copy-done.2), kind=kOutput, calls=%fused_computation.53 | convolution fusion | flops 1132462080 | bytes 9142272 | tf_op jit(solution)/shard_map/fhwc,cd->fhwd/dot_general | solution.py:33
  105.8 4.5 %fusion.27 = f32[4,6,160,384]{3,2,1,0:T(8,128)} fusion(bf16[4,6,160,384]{3,2,1,0:T(8,128)(2,1)S(1)} %fusion.8, bf16[3,3,3,384,384]{4,3,2,1,0:T(8,128)(2,1)S(1)} %copy-done.2), kind=kOutput, calls=%fused_computation.54 | convolution fusion | flops 1132462080 | bytes 9142272 | tf_op jit(solution)/shard_map/fhwc,cd->fhwd/dot_general | solution.py:33
  110.3 4.4 %fusion.28 = f32[4,6,160,384]{3,2,1,0:T(8,128)} fusion(bf16[4,6,160,384]{3,2,1,0:T(8,128)(2,1)S(1)} %fusion.8, bf16[3,3,3,384,384]{4,3,2,1,0:T(8,128)(2,1)S(1)} %copy-done.2), kind=kOutput, calls=%fused_computation.55 | convolution fusion | flops 1132462080 | bytes 9142272 | tf_op jit(solution)/shard_map/fhwc,cd->fhwd/dot_general | solution.py:33
  114.7 4.9 %fusion.29 = f32[4,6,160,384]{3,2,1,0:T(8,128)} fusion(bf16[4,6,160,384]{3,2,1,0:T(8,128)(2,1)S(1)} %fusion.8, bf16[3,3,3,384,384]{4,3,2,1,0:T(8,128)(2,1)S(1)} %copy-done.2), kind=kOutput, calls=%fused_computation.56 | convolution fusion | flops 1132462080 | bytes 9142272 | tf_op jit(solution)/shard_map/fhwc,cd->fhwd/dot_general | solution.py:33
  119.6 4.4 %fusion.30 = f32[4,6,160,384]{3,2,1,0:T(8,128)} fusion(bf16[4,6,160,384]{3,2,1,0:T(8,128)(2,1)S(1)} %fusion.8, bf16[3,3,3,384,384]{4,3,2,1,0:T(8,128)(2,1)S(1)} %copy-done.2), kind=kOutput, calls=%fused_computation.57 | convolution fusion | flops 1132462080 | bytes 9142272 | tf_op jit(solution)/shard_map/fhwc,cd->fhwd/dot_general | solution.py:33
  124.0 4.5 %fusion.31 = f32[4,6,160,384]{3,2,1,0:T(8,128)} fusion(bf16[4,6,160,384]{3,2,1,0:T(8,128)(2,1)S(1)} %fusion.8, bf16[3,3,3,384,384]{4,3,2,1,0:T(8,128)(2,1)S(1)} %copy-done.2), kind=kOutput, calls=%fused_computation.58 | convolution fusion | flops 1132462080 | bytes 9142272 | tf_op jit(solution)/shard_map/fhwc,cd->fhwd/dot_general | solution.py:33
  128.5 4.5 %fusion.32 = f32[4,6,160,384]{3,2,1,0:T(8,128)} fusion(bf16[4,6,160,384]{3,2,1,0:T(8,128)(2,1)S(1)} %fusion.8, bf16[3,3,3,384,384]{4,3,2,1,0:T(8,128)(2,1)S(1)} %copy-done.2), kind=kOutput, calls=%fused_computation.59 | convolution fusion | flops 1132462080 | bytes 9142272 | tf_op jit(solution)/shard_map/fhwc,cd->fhwd/dot_general | solution.py:33
  133.0 4.5 %fusion.33 = f32[4,6,160,384]{3,2,1,0:T(8,128)} fusion(bf16[4,6,160,384]{3,2,1,0:T(8,128)(2,1)S(1)} %fusion.8, bf16[3,3,3,384,384]{4,3,2,1,0:T(8,128)(2,1)S(1)} %copy-done.2), kind=kOutput, calls=%fused_computation.60 | convolution fusion | flops 1132462080 | bytes 9142272 | tf_op jit(solution)/shard_map/fhwc,cd->fhwd/dot_general | solution.py:33
  137.5 4.5 %fusion.48 = f32[4,6,160,384]{3,2,1,0:T(8,128)} fusion(bf16[4,6,160,384]{3,2,1,0:T(8,128)(2,1)S(1)} %fusion.8, bf16[3,3,3,384,384]{4,3,2,1,0:T(8,128)(2,1)S(1)} %copy-done.2), kind=kOutput, calls=%fused_computation.78 | convolution fusion | flops 849346560 | bytes 9142272 | tf_op jit(solution)/shard_map/fhwc,cd->fhwd/dot_general | solution.py:33
  141.9 4.6 %fusion.58 = f32[4,6,160,384]{3,2,1,0:T(8,128)} fusion(bf16[4,6,160,384]{3,2,1,0:T(8,128)(2,1)S(1)} %fusion.8, bf16[3,3,3,384,384]{4,3,2,1,0:T(8,128)(2,1)S(1)} %copy-done.2), kind=kOutput, calls=%fused_computation.88 | convolution fusion | flops 566231040 | bytes 9142272 | tf_op jit(solution)/shard_map/fhwc,cd->fhwd/dot_general | solution.py:33
  146.5 0.0 copy-start.3
  146.6 4.5 %fusion.38 = f32[4,6,160,384]{3,2,1,0:T(8,128)} fusion(bf16[4,6,160,384]{3,2,1,0:T(8,128)(2,1)S(1)} %fusion.8, bf16[3,3,3,384,384]{4,3,2,1,0:T(8,128)(2,1)S(1)} %copy-done.2), kind=kOutput, calls=%fused_computation.68 | convolution fusion | flops 1132462080 | bytes 9142272 | tf_op jit(solution)/shard_map/fhwc,cd->fhwd/dot_general | solution.py:33
  151.0 0.0 copy-done.3
  151.0 0.0 copy-start.4
  151.0 49.2 %fusion.9 = bf16[4,6,160,384]{3,2,1,0:T(8,128)(2,1)} fusion(f32[4,6,160,384]{3,2,1,0:T(8,128)} %fusion.33, f32[4,6,160,384]{3,2,1,0:T(8,128)} %fusion.32, f32[4,6,160,384]{3,2,1,0:T(8,128)} %fusion.31, f32[4,6,160,384]{3,2,1,0:T(8,128)} %fusion.38, f32[4,6,160,384]{3,2,1,0:T(8,128)} %fusion.30, f32[4,6,160,384]{3,2,1,0:T(8,128)} %fusion.29, ...), kind=kOutput, calls=%fused_computation.36 | convolution fusion | flops 1178173440 | bytes 162498048 | tf_op jit(solution)/shard_map/fhwc,cd->fhwd/dot_general | solution.py:33
  200.2 1.7 fusion.115
  201.9 1.9 collective-permute-start.1
  203.9 0.0 copy-done.4
  203.9 0.6 dynamic_slice.10
  205.8 0.7 broadcast_subtract_fusion
  206.4 8.5 %collective-permute-done.1 = bf16[4,2,160,384]{3,2,1,0:T(8,128)(2,1)S(1)} collective-permute-done((bf16[4,2,160,384]{3,2,1,0:T(8,128)(2,1)S(1)}, bf16[4,2,160,384]{3,2,1,0:T(8,128)(2,1)S(1)}, u32[]{:S(2)}, u32[]{:S(2)}) %collective-permute-start.1) | collective-permute-done | bytes 983072 | tf_op jit(solution)/shard_map/ppermute | solution.py:12
  214.9 1.7 add_convert_fusion
  216.5 1.5 pad_maximum_fusion.1
  (2 shorter events, 0.0 us)
Async XLA Ops:
  0.0 27.0 %collective-permute-start = (bf16[4,4,160,384]{3,2,1,0:T(8,128)(2,1)}, bf16[4,4,160,384]{3,2,1,0:T(8,128)(2,1)S(1)}, u32[]{:S(2)}, u32[]{:S(2)}) collective-permute-start(bf16[4,4,160,384]{3,2,1,0:T(8,128)(2,1)} %param.6), channel_id=1, source_target_pairs={{1,0},{2,1},{3,2},{4,3},{5,4},{6,5},{7,6},{8,7},{9,8},{10,9},{11,1... | collective-permute-start | bytes 5898248 | tf_op jit(solution)/shard_map/ppermute | solution.py:12
  4.0 26.0 %copy-start = (bf16[4,4,160,384]{3,2,1,0:T(8,128)(2,1)S(1)}, bf16[4,4,160,384]{3,2,1,0:T(8,128)(2,1)}, u32[]{:S(2)}) copy-start(bf16[4,4,160,384]{3,2,1,0:T(8,128)(2,1)} %param.6) | copy-start | bytes 5898244
  4.0 30.1 %copy-start.2 = (bf16[3,3,3,384,384]{4,3,2,1,0:T(8,128)(2,1)S(1)}, bf16[3,3,3,384,384]{4,3,2,1,0:T(8,128)(2,1)}, u32[]{:S(2)}) copy-start(bf16[3,3,3,384,384]{4,3,2,1,0:T(8,128)(2,1)} %param.8) | copy-start | bytes 23887876
  27.2 11.4 %copy-start.1 = (bf16[4,2,160,384]{3,2,1,0:T(8,128)(2,1)}, bf16[4,2,160,384]{3,2,1,0:T(8,128)(2,1)S(1)}, u32[]{:S(2)}) copy-start(bf16[4,2,160,384]{3,2,1,0:T(8,128)(2,1)S(1)} %slice.235) | copy-start | bytes 2949124
  146.5 4.5 %copy-start.3 = (f32[384]{0:T(512)S(1)}, f32[384]{0:T(512)}, u32[]{:S(2)}) copy-start(f32[384]{0:T(512)} %param.9) | copy-start | bytes 4612
  151.0 52.9 %copy-start.4 = (s32[16]{0:T(128)S(1)}, s32[16]{0:T(128)}, u32[]{:S(2)}) copy-start(s32[16]{0:T(128)} %param.11) | copy-start | bytes 196
  201.9 12.9 %collective-permute-start.1 = (bf16[4,2,160,384]{3,2,1,0:T(8,128)(2,1)S(1)}, bf16[4,2,160,384]{3,2,1,0:T(8,128)(2,1)S(1)}, u32[]{:S(2)}, u32[]{:S(2)}) collective-permute-start(bf16[4,2,160,384]{3,2,1,0:T(8,128)(2,1)S(1)} %get-tuple-element.7), channel_id=1, source_target_pairs={{0,1},{1,2},{2,3},{3,4},{4,5},{5,6},{6,7},{7,8},{8,9},{9,10},{10,1... | collective-permute-start | bytes 2949128 | tf_op jit(solution)/shard_map/ppermute | solution.py:12
where the time goes:
time: 222 us; the launch traced here: 218 us
  matrix products  166 us (75%)
  waiting for transfers between devices  31.5 us (14%)
  other arithmetic  10.7 us (5%)
  starting transfers between devices  3.88 us (2%)
  local copies, waits for them, and re-layouts  3.76 us (2%)
  between operations  2.28 us (1%)
    dot_general x27, matrix products, convolve(): jnp.einsum('fhwc,cd->fhwd', slab, weight[step_t, step_h, step_w], preferr...  166 us
    ppermute x2, waiting for transfers between devices, shifted(): return lax.ppermute(block, axis, route)  31.5 us
  transfers between devices with their start and end apart: 2, of which 2 were waited for; matrix products, arithmetic and copies ran while one was open for 1% of the time, Pallas kernels for 0%

commit v1 on v0

v1 whole, which is shorter than its diff:
```python
import jax
import jax.numpy as jnp
from jax import lax
from jax.experimental import pallas as pl
from jax.experimental.pallas import tpu as pltpu
from jax.sharding import PartitionSpec as P

F32 = jnp.float32
BF16 = jnp.bfloat16
TAPS = 3


def shifted(block, axis, distance):
    devices = range(lax.axis_size(axis))
    route = [(i - distance, i) for i in devices if i - distance in devices]
    return lax.ppermute(block, axis, route)


def coefficients(inter_ref, ramp_ref, chans):
    index = lax.axis_index("rows")
    count = lax.axis_size("rows")
    previous = jnp.maximum(index - 1, 0)
    own = jnp.where(index == count - 1, 0, inter_ref[index])
    before = jnp.where(index > 0, inter_ref[previous], 0)
    row = lambda scalar: jnp.full((1, chans), scalar, jnp.int32)
    own, before, ramp = row(own), row(before), row(ramp_ref[previous])
    steps = (ramp + 1).astype(F32)
    first = jnp.where(before > 0, jnp.maximum(ramp, 0).astype(F32) / steps, 0.0)
    second = jnp.where(before > 1, jnp.maximum(ramp - 1, 0).astype(F32) / steps, 0.0)
    top = first
    below_first = jnp.where(before > 1, 1.0, 1.0 - first)
    below_second = 1.0 - second
    bottom = jnp.where(own > 0, 1.0, 0.0)
    return top, below_first, below_second, bottom


def activate(values, gamma):
    square = jnp.mean(values * values, axis=-1, keepdims=True)
    normed = values * lax.rsqrt(square + 1e-06) * gamma
    half = 0.5 * normed
    return half + half * jnp.tanh(half)


def spread(act, line, targets):
    width, chans = act.shape
    line[8 : 8 + width] = act
    for step in range(TAPS):
        piece = act if step == 1 else line[7 + step : 7 + step + width]
        for target, scale in targets:
            part = piece.astype(BF16)
            if scale is not None:
                part = (part.astype(F32) * scale).astype(BF16)
            target[:, step * chans : (step + 1) * chans] = part


def interior(
    inter_ref, ramp_ref, x_hbm, w_hbm, gamma_ref, bias_ref,
    out_hbm, part_hbm,
    x_s, w_s, line, flat, scaled, acc, done_s, part_s, x_sem, w_sem, o_sem, p_sem,
):
    frames, rows, width, chans = x_s.shape
    deep = TAPS * chans
    x_in = [pltpu.make_async_copy(x_hbm.at[f], x_s.at[f], x_sem.at[f]) for f in range(frames)]
    x_in[0].start()
    w_in = {}
    for slot in range(TAPS):
        for kh in range(TAPS):
            w_in[slot, kh] = pltpu.make_async_copy(
                w_hbm.at[TAPS - 1 - slot, kh],
                w_s.at[pl.ds(kh * deep, deep), pl.ds(slot * chans, chans)],
                w_sem.at[slot, kh],
            )
    for kh in range(TAPS):
        w_in[0, kh].start()
    for f in range(1, frames):
        x_in[f].start()
    for slot in range(1, TAPS):
        for kh in range(TAPS):
            w_in[slot, kh].start()
    _, below_first, below_second, _ = coefficients(inter_ref, ramp_ref, chans)
    gamma = gamma_ref[...]
    bias = bias_ref[...]
    line[:, 0:8] = jnp.zeros((rows, 8, chans), F32)
    line[:, 8 + width : 16 + width] = jnp.zeros((rows, 8, chans), F32)

    def prepare(f):
        x_in[f].wait()
        for h in range(rows):
            act = activate(x_s[f, h].astype(F32), gamma)
            targets = [(flat.at[f, h], None)]
            if h == 1:
                targets.append((scaled.at[f, 0], below_first))
            if h == 2:
                targets.append((scaled.at[f, 1], below_second))
            spread(act, line.at[h], targets)

    copies = []
    for f in range(frames):
        prepare(f)
        if f == 0:
            for copy in w_in.values():
                copy.wait()
        wide = min(TAPS, frames - f) * chans
        weight = lambda low, high: w_s[low * deep : high * deep, :wide]
        for r in range(rows):
            if r == 0:
                left = jnp.concatenate([flat[f, 0], scaled[f, 0]], axis=1)
                right = weight(1, 3)
            elif r == rows - 1:
                left = jnp.concatenate([flat[f, r - 1], flat[f, r]], axis=1)
                right = weight(0, 2)
            else:
                last = scaled[f, 1] if r == 1 else flat[f, r + 1]
                left = jnp.concatenate([flat[f, r - 1], flat[f, r], last], axis=1)
                right = weight(0, 3)
            product = jnp.dot(left, right, preferred_element_type=F32)
            for slot in range(min(TAPS, frames - f)):
                g = f + slot
                term = product[:, slot * chans : (slot + 1) * chans]
                if f == 0 or slot == 2:
                    acc[g, r] = term
                else:
                    acc[g, r] += term
        for r in range(rows):
            total = acc[f, r] + (x_s[f, r].astype(F32) + bias)
            if r == 0:
                part_s[f, 0] = total
            elif r == rows - 1:
                part_s[f, 1] = total
            else:
                done_s[f, r - 1] = total.astype(BF16)
        copies.append(pltpu.make_async_copy(
            done_s.at[f], out_hbm.at[f, pl.ds(1, rows - 2)], o_sem.at[f]))
        copies[-1].start()
        copies.append(pltpu.make_async_copy(part_s.at[f], part_hbm.at[f], p_sem.at[f]))
        copies[-1].start()
    for copy in copies:
        copy.wait()


def edges(
    inter_ref, ramp_ref, top_hbm, bottom_hbm, w_hbm, gamma_ref, part_hbm, _,
    out_hbm,
    h_s, w_s, line, flat, acc, part_s, done_s, h_sem, w_sem, p_sem, o_sem,
):
    _, frames, width, chans = h_s.shape
    deep = TAPS * chans
    rows = out_hbm.shape[1]
    h_in = [
        pltpu.make_async_copy(source, h_s.at[side], h_sem.at[side])
        for side, source in enumerate((top_hbm, bottom_hbm))
    ]
    for copy in h_in:
        copy.start()
    w_in = []
    for side in range(2):
        for slot in range(TAPS):
            w_in.append(pltpu.make_async_copy(
                w_hbm.at[TAPS - 1 - slot, 2 * side],
                w_s.at[side, :, pl.ds(slot * chans, chans)],
                w_sem.at[side, slot],
            ))
            w_in[-1].start()
    p_in = pltpu.make_async_copy(part_hbm, part_s, p_sem)
    p_in.start()
    top, _, _, bottom = coefficients(inter_ref, ramp_ref, chans)
    gamma = gamma_ref[...]
    line[:, 0:8] = jnp.zeros((2, 8, chans), F32)
    line[:, 8 + width : 16 + width] = jnp.zeros((2, 8, chans), F32)
    for copy in h_in:
        copy.wait()
    for f in range(frames):
        for side, scale in enumerate((top, bottom)):
            act = activate(h_s[side, f].astype(F32), gamma)
            spread(act, line.at[side], [(flat.at[side, f], scale)])
    for copy in w_in:
        copy.wait()
    p_in.wait()
    copies = []
    for side in range(2):
        for f in range(frames):
            count = min(TAPS, frames - f)
            product = jnp.dot(
                flat[side, f], w_s[side, :, : count * chans], preferred_element_type=F32
            )
            for slot in range(count):
                part_s[f + slot, side] += product[:, slot * chans : (slot + 1) * chans]
            done_s[f, side] = part_s[f, side].astype(BF16)
            copies.append(pltpu.make_async_copy(
                done_s.at[f, side], out_hbm.at[f, side * (rows - 1)], o_sem.at[f, side]))
            copies[-1].start()
    for copy in copies:
        copy.wait()


def per_device(latents, gamma, weight, bias, intersection, ramp):
    frames, rows, width, chans = latents.shape
    deep = TAPS * chans
    gamma = gamma.reshape(1, chans)
    bias = bias.reshape(1, chans)
    weight = weight.reshape(TAPS, TAPS, deep, chans)
    top = shifted(latents[:, rows - 1], "rows", 1)
    bottom = shifted(latents[:, 0], "rows", -1)
    smem = pl.BlockSpec(memory_space=pltpu.SMEM)
    vmem = pl.BlockSpec(memory_space=pltpu.VMEM)
    hbm = pl.BlockSpec(memory_space=pl.ANY)
    dma = pltpu.SemaphoreType.DMA
    out, part = pl.pallas_call(
        interior,
        out_shape=(
            jax.ShapeDtypeStruct(latents.shape, BF16),
            jax.ShapeDtypeStruct((frames, 2, width, chans), F32),
        ),
        in_specs=[smem, smem, hbm, hbm, vmem, vmem],
        out_specs=(hbm, hbm),
        scratch_shapes=[
            pltpu.VMEM((frames, rows, width, chans), BF16),
            pltpu.VMEM((TAPS * deep, TAPS * chans), BF16),
            pltpu.VMEM((rows, width + 16, chans), F32),
            pltpu.VMEM((frames, rows, width, deep), BF16),
            pltpu.VMEM((frames, 2, width, deep), BF16),
            pltpu.VMEM((frames, rows, width, chans), F32),
            pltpu.VMEM((frames, rows - 2, width, chans), BF16),
            pltpu.VMEM((frames, 2, width, chans), F32),
            dma((frames,)),
            dma((TAPS, TAPS)),
            dma((frames,)),
            dma((frames,)),
        ],
        cost_estimate=pl.CostEstimate(
            flops=2 * 90 * width * deep * chans, bytes_accessed=14 * 2**20, transcendentals=0
        ),
        compiler_params=pltpu.CompilerParams(vmem_limit_bytes=50 * 2**20),
        name="interior",
    )(intersection, ramp, latents, weight, gamma, bias)
    return pl.pallas_call(
        edges,
        out_shape=jax.ShapeDtypeStruct(latents.shape, BF16),
        in_specs=[smem, smem, hbm, hbm, hbm, vmem, hbm, hbm],
        out_specs=hbm,
        input_output_aliases={7: 0},
        scratch_shapes=[
            pltpu.VMEM((2, frames, width, chans), BF16),
            pltpu.VMEM((2, deep, TAPS * chans), BF16),
            pltpu.VMEM((2, width + 16, chans), F32),
            pltpu.VMEM((2, frames, width, deep), BF16),
            pltpu.VMEM((8, 128), F32),
            pltpu.VMEM((frames, 2, width, chans), F32),
            pltpu.VMEM((frames, 2, width, chans), BF16),
            dma((2,)),
            dma((2, TAPS)),
            dma(()),
            dma((frames, 2)),
        ],
        cost_estimate=pl.CostEstimate(
            flops=2 * 18 * width * deep * chans, bytes_accessed=9 * 2**20, transcendentals=0
        ),
        compiler_params=pltpu.CompilerParams(vmem_limit_bytes=40 * 2**20),
        name="edges",
    )(intersection, ramp, top, bottom, weight, gamma, part, out)


def solution(mesh):
    in_specs = (P("clips", "rows", None, None), P(), P(), P(), P("clips"), P("clips"))
    out_specs = P("clips", "rows", None, None)
    return jax.shard_map(
        per_device, mesh=mesh, in_specs=in_specs, out_specs=out_specs, check_vma=False
    )
```

time: 222 us -> 39.6 us (0.18); the launches traced: 218 us -> 39.5 us
  matrix products: 166 us -> 0 us
  waiting for transfers between devices: 31.5 us -> 0.01 us
  Pallas kernels: 0 us -> 31.2 us
  other arithmetic: 10.7 us -> 0.01 us
  starting transfers between devices: 3.88 us -> 6.46 us
  local copies, waits for them, and re-layouts: 3.76 us -> 1.46 us
    dot_general x27 -> x0, matrix products: 166 us -> none  [convolve(): jnp.einsum('fhwc,cd->fhwd', slab, weight[step_t, step_h, step_w], preferr...]
    ppermute x2, waiting for transfers between devices: 31.5 us -> 0.01 us  [shifted(): return lax.ppermute(block, axis, route)]
    pallas_call x0 -> x2, Pallas kernels: none -> 31.2 us  [the longest x1 23.1 us: per_device(): pl.pallas_call(interior, out_shape=(jax.ShapeDtypeStruct(latents.shape, B...]
    convert_element_type x3 -> x0, other arithmetic: 5.71 us -> none  [the longest x1 4.05 us: activate(): return (jax.nn.silu(normed) * keep).astype(jnp.bfloat16)]
    reduce_sum x1 -> x0, other arithmetic: 2.8 us -> none  [activate(): square = jnp.mean(values * values, axis=-1, keepdims=True)]
    ppermute x2, starting transfers between devices: 3.88 us -> 6.46 us  [shifted(): return lax.ppermute(block, axis, route)]
  transfers between devices with their start and end apart: 2 -> 2, of which waited for: 2 -> 0; matrix products, arithmetic and copies ran while one was open for 1% -> 0% of each run, Pallas kernels for 0% -> 58%
where the time goes in v1:
time: 39.6 us; the launch traced here: 39.5 us
  Pallas kernels  31.2 us (79%)
  starting transfers between devices  6.46 us (16%)
  local copies, waits for them, and re-layouts  1.46 us (4%)
    pallas_call x1, Pallas kernels, per_device(): pl.pallas_call(interior, out_shape=(jax.ShapeDtypeStruct(latents.shape, B...  23.1 us
    pallas_call x1, Pallas kernels, per_device(): pl.pallas_call(edges, out_shape=jax.ShapeDtypeStruct(latents.shape, BF16)...  8.13 us
    ppermute x2, starting transfers between devices, shifted(): return lax.ppermute(block, axis, route)  6.46 us
    squeeze x1, local copies, waits for them, and re-layouts, per_device(): bottom = shifted(latents[:, 0], 'rows', -1)  1.42 us
  transfers between devices with their start and end apart: 2, of which 0 were waited for; matrix products, arithmetic and copies ran while one was open for 0% of the time, Pallas kernels for 58%

profile of v1, /device:TPU:1, one launch (start us, length us, event | category | flops | bytes accessed | tf_op | source)
XLA Modules:
  0.0 39.5 jit_solution(16949402932265860087)
XLA Ops:
  0.0 0.0 copy-start
  0.0 0.0 copy-start.3
  0.0 0.0 copy-start.4
  0.0 0.0 copy-start.2
  0.0 0.0 copy-start.1
  0.0 1.4 %slice_bitcast_fusion = (bf16[4,160,384]{2,1,0:T(8,128)(2,1)S(1)}, bf16[4,160,384]{2,1,0:T(8,128)(2,1)S(1)}) fusion(bf16[4,4,160,384]{3,2,1,0:T(8,128)(2,1)} %x_hbm.1), kind=kLoop, calls=%fused_computation | loop fusion | bytes 1966080 | tf_op jit(solution)/shard_map/squeeze | solution.py:203
  1.5 2.0 %collective-permute-start.1 = (bf16[4,160,384]{2,1,0:T(8,128)(2,1)S(1)}, bf16[4,160,384]{2,1,0:T(8,128)(2,1)S(1)}, u32[]{:S(2)}, u32[]{:S(2)}) collective-permute-start(bf16[4,160,384]{2,1,0:T(8,128)(2,1)S(1)} %get-tuple-element.9), channel_id=1, source_target_pairs={{1,0},{2,1},{3,2},{4,3},{5,4},{6,5},{7,6},{8,7},{9,8},{10,9},{11,1... | collective-permute-start | bytes 1474568 | tf_op jit(solution)/shard_map/ppermute | solution.py:16
  3.4 4.5 %collective-permute-start = (bf16[4,160,384]{2,1,0:T(8,128)(2,1)S(1)}, bf16[4,160,384]{2,1,0:T(8,128)(2,1)S(1)}, u32[]{:S(2)}, u32[]{:S(2)}) collective-permute-start(bf16[4,160,384]{2,1,0:T(8,128)(2,1)S(1)} %get-tuple-element.10), channel_id=1, source_target_pairs={{0,1},{1,2},{2,3},{3,4},{4,5},{5,6},{6,7},{7,8},{8,9},{9,10},{10,1... | collective-permute-start | bytes 1474568 | tf_op jit(solution)/shard_map/ppermute | solution.py:16
  7.9 0.0 copy-done.3
  7.9 0.0 copy-done.4
  8.0 0.0 slice-start
  8.0 0.0 copy-done
  8.0 0.0 copy-done.2
  8.0 0.0 copy-done.1
  8.0 0.0 slice-start.1
  8.0 23.1 %interior.1 = (bf16[4,4,160,384]{3,2,1,0:T(8,128)(2,1)}, f32[4,2,160,384]{3,2,1,0:T(8,128)S(1)}) custom-call(s32[16]{0:T(128)S(1)} %copy-done.1, s32[16]{0:T(128)S(1)} %copy-done.2, bf16[4,4,160,384]{3,2,1,0:T(8,128)(2,1)S(1)} %copy-done, bf16[3,3,1152,384]{3,2,1,0:T(8,128)(2,1)} %bitcast.9, f32[1,384]{1,0:T(1,128)S(1)} %reshape.10.gamma_ref, ...), custom_call_target="tpu_custom_call" | custom-call | flops 12740198400 | bytes 14680064 | tf_op jit(solution)/shard_map/interior/pallas_call | solution.py:208
  31.1 0.0 collective-permute-done.1.bottom_hbm
  31.1 0.0 collective-permute-done.top_hbm
  31.1 0.0 slice-done
  31.1 0.0 slice-done.1
  31.2 8.1 %edges.1 = bf16[4,4,160,384]{3,2,1,0:T(8,128)(2,1)} custom-call(s32[16]{0:T(128)S(1)} %copy-done.1, s32[16]{0:T(128)S(1)} %copy-done.2, bf16[4,160,384]{2,1,0:T(8,128)(2,1)S(1)} %collective-permute-done.top_hbm, bf16[4,160,384]{2,1,0:T(8,128)(2,1)S(1)} %collective-permute-done.1.bottom_hbm, ...), custom_call_target="tpu_custom_call", output_to_operand_aliasing={{}: (7, {})} | custom-call | flops 2548039680 | bytes 9437184 | tf_op jit(solution)/shard_map/edges/pallas_call | solution.py:236
  (3 shorter events, 0.0 us)
Async XLA Ops:
  0.0 8.0 %copy-start = (bf16[4,4,160,384]{3,2,1,0:T(8,128)(2,1)S(1)}, bf16[4,4,160,384]{3,2,1,0:T(8,128)(2,1)}, u32[]{:S(2)}) copy-start(bf16[4,4,160,384]{3,2,1,0:T(8,128)(2,1)} %x_hbm.1) | copy-start | bytes 5898244
  0.0 7.9 %copy-start.3 = (f32[384]{0:T(512)S(1)}, f32[384]{0:T(512)}, u32[]{:S(2)}) copy-start(f32[384]{0:T(512)} %param.7) | copy-start | bytes 4612
  0.0 7.9 %copy-start.4 = (f32[384]{0:T(512)S(1)}, f32[384]{0:T(512)}, u32[]{:S(2)}) copy-start(f32[384]{0:T(512)} %param.9) | copy-start | bytes 4612
  0.0 8.0 %copy-start.2 = (s32[16]{0:T(128)S(1)}, s32[16]{0:T(128)}, u32[]{:S(2)}) copy-start(s32[16]{0:T(128)} %ramp_ref.3) | copy-start | bytes 196
  0.0 8.0 %copy-start.1 = (s32[16]{0:T(128)S(1)}, s32[16]{0:T(128)}, u32[]{:S(2)}) copy-start(s32[16]{0:T(128)} %inter_ref.3) | copy-start | bytes 196
  1.5 29.7 %collective-permute-start.1 = (bf16[4,160,384]{2,1,0:T(8,128)(2,1)S(1)}, bf16[4,160,384]{2,1,0:T(8,128)(2,1)S(1)}, u32[]{:S(2)}, u32[]{:S(2)}) collective-permute-start(bf16[4,160,384]{2,1,0:T(8,128)(2,1)S(1)} %get-tuple-element.9), channel_id=1, source_target_pairs={{1,0},{2,1},{3,2},{4,3},{5,4},{6,5},{7,6},{8,7},{9,8},{10,9},{11,1... | collective-permute-start | bytes 1474568 | tf_op jit(solution)/shard_map/ppermute | solution.py:16
  3.4 27.7 %collective-permute-start = (bf16[4,160,384]{2,1,0:T(8,128)(2,1)S(1)}, bf16[4,160,384]{2,1,0:T(8,128)(2,1)S(1)}, u32[]{:S(2)}, u32[]{:S(2)}) collective-permute-start(bf16[4,160,384]{2,1,0:T(8,128)(2,1)S(1)} %get-tuple-element.10), channel_id=1, source_target_pairs={{0,1},{1,2},{2,3},{3,4},{4,5},{5,6},{6,7},{7,8},{8,9},{9,10},{10,1... | collective-permute-start | bytes 1474568 | tf_op jit(solution)/shard_map/ppermute | solution.py:16
  8.0 23.2 %slice-start = ((s8[7962624]{0:T(1024)(128)(4,1)}), s8[4194304]{0:T(1024)(128)(4,1)S(1)}, s32[]{:S(2)}) async-start(s8[7962624]{0:T(1024)(128)(4,1)} %bitcast.10), calls=%async_computation | async-start | bytes 8388608
  8.0 23.1 %slice-start.1 = ((s8[7962624]{0:T(1024)(128)(4,1)}), s8[3768320]{0:T(1024)(128)(4,1)S(1)}, s32[]{:S(2)}) async-start(s8[7962624]{0:T(1024)(128)(4,1)} %bitcast.10), calls=%async_computation.1 | async-start | bytes 7536640

commit v2 on v0

v2 whole, which is shorter than its diff:
```python
import jax
import jax.numpy as jnp
from jax import lax
from jax.experimental import pallas as pl
from jax.experimental.pallas import tpu as pltpu
from jax.sharding import PartitionSpec as P

F32 = jnp.float32
BF16 = jnp.bfloat16
TAPS = 3
LANES = 128
SIDE = 256
CHUNK = 32
MXUS = 2
ACCS = 6


def scales(inter_ref, ramp_ref):
    index = lax.axis_index("rows")
    count = lax.axis_size("rows")
    previous = jnp.maximum(index - 1, 0)
    own = jnp.where(index == count - 1, 0, inter_ref[index])
    before = jnp.where(index > 0, inter_ref[previous], 0)
    row = lambda scalar: jnp.full((1, LANES), scalar, jnp.int32)
    own, before, ramp = row(own), row(before), row(ramp_ref[previous])
    steps = (ramp + 1).astype(F32)
    first = jnp.where(before > 0, jnp.maximum(ramp, 0).astype(F32) / steps, 0.0)
    second = jnp.where(before > 1, jnp.maximum(ramp - 1, 0).astype(F32) / steps, 0.0)
    below_first = jnp.where(before > 1, 1.0, 1.0 - first)
    bottom = jnp.where(own > 0, 1.0, 0.0)
    return first, below_first, 1.0 - second, bottom


def parity():
    return lax.rem(lax.axis_index("rows"), 2)


def activate(values, gamma):
    square = jnp.mean(values * values, axis=-1, keepdims=True)
    normed = values * lax.rsqrt(square + 1e-06) * gamma
    half = 0.5 * normed
    return half + half * jnp.tanh(half)


def prepare(source, gamma, line, target):
    width, chans = source.shape

    def first(at):
        act = activate(source[at : at + CHUNK].astype(F32), gamma)
        line[8 + at : 8 + at + CHUNK] = act
        target[at : at + CHUNK, chans : 2 * chans] = act.astype(BF16)

    def second(at):
        for step in (0, 2):
            piece = line[7 + step + at : 7 + step + at + CHUNK]
            target[at : at + CHUNK, step * chans : (step + 1) * chans] = piece.astype(BF16)

    for at in range(0, width, CHUNK):
        yield lambda at=at: first(at)
    for at in range(0, width, CHUNK):
        yield lambda at=at: second(at)


def clear_ends(line):
    lines, padded, chans = line.shape
    line[:, 0:8] = jnp.zeros((lines, 8, chans), F32)
    line[:, padded - 8 : padded] = jnp.zeros((lines, 8, chans), F32)


class Queue:
    def __init__(self):
        self.items = []
        self.done = 0

    def add(self, steps):
        self.items.extend(steps)
        return len(self.items)

    def until(self, mark):
        while self.done < mark:
            self.items[self.done]()
            self.done += 1

    def some(self, number):
        self.until(min(len(self.items), self.done + number))


def tiles_of(chans, count):
    blocks = [(slot, block) for slot in range(count) for block in range(chans // LANES)]
    return [blocks[i : i + 2] for i in range(0, len(blocks), 2)]


def jobs_of(tiles, rows):
    full = range(rows)
    jobs = [
        [(tiles[i], full), (tiles[i + 1], full)] for i in range(0, len(tiles) - 1, 2)
    ]
    if len(tiles) % 2:
        jobs.append([(tiles[-1], full[: rows // 2]), (tiles[-1], full[rows // 2 :])])
    return jobs


def in_pairs(chunks):
    return [chunks[i : i + 2] for i in range(0, len(chunks), 2)]


def cells(w_ref, tile, places):
    columns = []
    for slot, block in tile:
        parts = [
            w_ref[TAPS - 1 - slot, kh, rest * LANES : (rest + 1) * LANES,
                  block * LANES : (block + 1) * LANES]
            for kh, rest in places
        ]
        while len(parts) < 2:
            parts.append(jnp.zeros((LANES, LANES), BF16))
        columns.append(jnp.concatenate(parts, axis=0))
    while len(columns) < 2:
        columns.append(jnp.zeros((SIDE, LANES), BF16))
    return jnp.concatenate(columns, axis=1)


def beside(parts):
    while len(parts) < 2:
        parts = parts + [jnp.zeros_like(parts[0])]
    return jnp.concatenate(parts, axis=1)


class Units:
    def __init__(self, accs):
        self.accs = [accs[m * ACCS : (m + 1) * ACCS] for m in range(MXUS)]
        self.stage = [0] * MXUS
        self.load = [None] * MXUS

    def weights(self, m, operand):
        pltpu.matmul_push_rhs(operand, self.stage[m], m)
        self.load[m] = self.stage[m]
        self.stage[m] = 1 - self.stage[m]

    def add(self, m, number, block):
        pltpu.matmul_acc_lhs(self.accs[m][number], block, self.load[m])
        self.load[m] = None

    def pop(self, m, number):
        return pltpu.matmul_pop(self.accs[m][number])


def conv_passes(depth):
    return in_pairs([divmod(chunk, depth) for chunk in range(TAPS * depth)])


def acc_of(r, places, rows):
    if not any(0 <= r + kh - 1 < rows for kh, _ in places):
        return None
    if r < 2 and places[-1][0] == 2:
        return 4 + r
    return r


def row_block(flat_row, r, places):
    parts = []
    for kh, rest in places:
        h = r + kh - 1
        if h < 0:
            parts.append(jnp.zeros((flat_row(0).shape[0], LANES), BF16))
        else:
            parts.append(flat_row(h)[:, rest * LANES : (rest + 1) * LANES])
    return beside(parts)


def matrix_job(units, job, passes, rows, flat_row, weight, step, pop, between=None):
    for number, places in enumerate(passes):
        active = [
            (m, tile, [r for r in rows_of if acc_of(r, places, rows) is not None])
            for m, (tile, rows_of) in enumerate(job)
        ]
        for m, tile, rows_of in active:
            if rows_of:
                units.weights(m, weight(tile, places))
        for r in (3, 1, 2, 0):
            if any(r in rows_of for _, _, rows_of in active):
                block = row_block(flat_row, r, places)
                for m, _, rows_of in active:
                    if r in rows_of:
                        units.add(m, acc_of(r, places, rows), block)
        if between is not None and number == len(passes) - 3:
            between()
        for r in (3, 1, 0, 2):
            here = acc_of(r, places, rows)
            later = [acc_of(r, other, rows) for other in passes[number + 1 :]]
            if here is not None and here not in later:
                last = all(other is None for other in later)
                for m, (tile, rows_of) in enumerate(job):
                    if r in rows_of:
                        pop(m, tile, here, r, last)
        step()


def select(x_hbm, far_ref, near_ref, sem):
    frames, rows = x_hbm.shape[:2]
    odd = parity()
    copies = []
    for place, (target, row) in enumerate(
        ((far_ref, odd * (rows - 1)), (near_ref, (1 - odd) * (rows - 1)))
    ):
        copies.append(pltpu.make_async_copy(x_hbm.at[:, row], target, sem.at[place]))
        copies[-1].start()
    for copy in copies:
        copy.wait()


def interior(
    inter_ref, ramp_ref, x_ref, near_ref, w_hbm, gamma_ref, bias_ref,
    out_hbm, part_ref, w_ref, last_ref, carry_ref, nacc_ref,
    line, flat, nflat, acc, done_s, w_sem, o_sem,
):
    frames, rows, width, chans = x_ref.shape
    depth = TAPS * chans // LANES
    passes = conv_passes(depth)
    order = [(slot, kh) for slots in ((0, 1), (2,)) for kh in range(TAPS) for slot in slots]
    w_in = {
        (slot, kh): pltpu.make_async_copy(
            w_hbm.at[TAPS - 1 - slot, kh], w_ref.at[TAPS - 1 - slot, kh], w_sem.at[slot, kh])
        for slot, kh in order
    }
    starts = [w_in[key].start for key in order]
    for start in starts[:4]:
        start()
    starts = starts[4:]
    _, below_first, below_second, _ = scales(inter_ref, ramp_ref)
    below = (below_first, below_second)
    gamma = gamma_ref[...]
    clear_ends(line)
    near_kh = 2 * (1 - parity())

    def flat_at(f, h):
        return last_ref.at[h] if f == frames - 1 else flat.at[f, h]

    queue = Queue()
    ready = {}
    for f in range(frames):
        for h in reversed(range(rows)):
            ready[f, h] = queue.add(
                prepare(x_ref.at[f, h], gamma, line.at[h], flat_at(f, h)))
        ready[f] = queue.add(prepare(near_ref.at[f], gamma, line.at[rows], nflat.at[f]))

    def weight(tile, places):
        for slot, _ in tile:
            for kh, _ in places:
                copy = w_in.pop((slot, kh), None)
                if copy is not None:
                    copy.wait()
        return cells(w_ref, tile, places)

    def contribute(g, r, lanes, term, first, final):
        if first:
            term = term + (x_ref[g, r, :, lanes].astype(F32) + bias_ref[:, lanes])
        else:
            term = term + acc[g, r, :, lanes]
        if not final:
            acc[g, r, :, lanes] = term
        elif r == 0:
            part_ref[g, 0, :, lanes] = term
        elif r == rows - 1:
            part_ref[g, 1, :, lanes] = term
        else:
            done_s[g, r - 1, :, lanes] = term.astype(BF16)

    def run(*accs):
        units = Units(accs)

        def pop(f, m, tile, number, r, last):
            product = units.pop(m, number)
            for i, (slot, block) in enumerate(tile):
                lanes = slice(block * LANES, (block + 1) * LANES)
                term = product[:, i * LANES : (i + 1) * LANES]
                if number >= 4:
                    term = term * below[r]
                contribute(
                    f + slot, r, lanes, term,
                    (f == 0 or slot == 2) and number < 4, slot == 0 and last)

        def near(f, job):
            queue.until(ready[f])
            for places in in_pairs([(near_kh, c) for c in range(depth)]):
                low, high = places[0][1] * LANES, (places[-1][1] + 1) * LANES
                for m, (tile, _) in enumerate(job):
                    if m == 0 or tile is not job[0][0]:
                        units.weights(m, cells(w_ref, tile, places))
                        block = nflat[f, :, low:high]
                        units.add(m, 0, block if len(places) == 2 else beside([block]))

        def near_pop(f, job):
            for m, (tile, _) in enumerate(job):
                if m == 0 or tile is not job[0][0]:
                    product = units.pop(m, 0)
                    for i, (slot, block) in enumerate(tile):
                        lanes = slice(block * LANES, (block + 1) * LANES)
                        term = product[:, i * LANES : (i + 1) * LANES]
                        if f > 0 and slot < 2:
                            term = term + nacc_ref[f + slot, :, lanes]
                        nacc_ref[f + slot, :, lanes] = term

        queue.until(ready[0, 3] if rows == 4 else ready[0, 0])
        for start in starts[:3]:
            start()
        queue.until(ready[0, 2] if rows == 4 else ready[0, 0])
        for start in starts[3:]:
            start()
        for f in range(frames - 1):
            jobs = jobs_of(tiles_of(chans, min(TAPS, frames - f)), rows)
            for place, job in enumerate(jobs):
                flat_row = lambda h: flat.at[f, h]
                if f == 0 and place == 0:
                    for r in reversed(range(rows)):
                        queue.until(ready[0, max(r - 1, 0)])
                        matrix_job(
                            units, [(tile, [r]) for tile, _ in job], passes, rows, flat_row,
                            weight, lambda: queue.some(1),
                            lambda *rest: pop(f, *rest))
                    near(f, job)
                    near_pop(f, job)
                else:
                    queue.until(ready[f])
                    matrix_job(
                        units, job, passes, rows, flat_row, weight,
                        lambda: queue.some(2), lambda *rest: pop(f, *rest),
                        lambda: near(f, job))
                    near_pop(f, job)
            copy = pltpu.make_async_copy(
                done_s.at[f], out_hbm.at[f, pl.ds(1, rows - 2)], o_sem.at[f])
            copy.start()
        f = frames - 1
        queue.until(ready[f])
        tiles = tiles_of(chans, 1)
        job = [(tile, None) for tile in tiles]
        near(f, job)
        near_pop(f, job)
        for r in range(rows):
            carry_ref[r] = acc[f, r]
        for f in range(frames - 1):
            pltpu.make_async_copy(
                done_s.at[f], out_hbm.at[f, pl.ds(1, rows - 2)], o_sem.at[f]).wait()

    pl.run_scoped(run, *[pltpu.ACC(m)((width, SIDE), F32) for m in range(MXUS) for _ in range(ACCS)])


def edges(
    inter_ref, ramp_ref, far_ref, w_ref, gamma_ref, part_ref, last_ref, carry_ref, nacc_ref, _,
    out_hbm,
    line, fflat, acc, facc, tail, done_s, inner_s, o_sem, i_sem,
):
    frames, width, chans = far_ref.shape
    rows = out_hbm.shape[1]
    depth = TAPS * chans // LANES
    passes = conv_passes(depth)
    odd = parity()
    top, below_first, below_second, bottom = scales(inter_ref, ramp_ref)
    below = (below_first, below_second)
    far_scale = jnp.where(odd == 1, bottom, top)
    near_scale = jnp.where(odd == 1, top, bottom)
    gamma = gamma_ref[...]
    clear_ends(line)
    final = frames - 1
    blocks = [slice(b * LANES, (b + 1) * LANES) for b in range(chans // LANES)]

    queue = Queue()
    ready = [
        queue.add(prepare(far_ref.at[f], gamma, line.at[0], fflat.at[f])) for f in range(frames)
    ]

    def near_row(g, at):
        span = slice(at, at + CHUNK)
        for lanes in blocks:
            base = tail[1 - odd, span, lanes] if g == final else part_ref[g, 1 - odd, span, lanes]
            total = base + near_scale * nacc_ref[g, span, lanes]
            done_s[g, 1 - odd, span, lanes] = total.astype(BF16)

    def run(*accs):
        units = Units(accs)

        def pop(m, tile, number, r, last):
            product = units.pop(m, number)
            for i, (_, block) in enumerate(tile):
                lanes = blocks[block]
                term = product[:, i * LANES : (i + 1) * LANES]
                if number >= 4:
                    term = acc[r, :, lanes] + term * below[r]
                else:
                    term = carry_ref[r, :, lanes] + term
                if not last:
                    acc[r, :, lanes] = term
                elif r == 0 or r == rows - 1:
                    tail[0 if r == 0 else 1, :, lanes] = term
                else:
                    inner_s[r - 1, :, lanes] = term.astype(BF16)

        tiles = tiles_of(chans, 1)
        job = [(tile, range(rows)) for tile in tiles]
        matrix_job(
            units, job, passes, rows, lambda h: last_ref.at[h],
            lambda tile, places: cells(w_ref, tile, places), lambda: queue.some(2), pop)
        inner = pltpu.make_async_copy(
            inner_s, out_hbm.at[final, pl.ds(1, rows - 2)], i_sem)
        inner.start()
        for g in range(frames):
            queue.add([lambda g=g, at=at: near_row(g, at) for at in range(0, width, CHUNK)])
        whole = [
            (f, tile) for f in range(frames) for tile in tiles_of(chans, min(TAPS, frames - f))
        ]
        for number, pair in enumerate(in_pairs(whole)):
            queue.until(ready[max(f for f, _ in pair)])
            here = (number % 2) * 3
            for places in in_pairs([(2 * odd, c) for c in range(depth)]):
                low, high = places[0][1] * LANES, (places[-1][1] + 1) * LANES
                for m, (f, tile) in enumerate(pair):
                    units.weights(m, cells(w_ref, tile, places))
                for m, (f, tile) in enumerate(pair):
                    block = fflat[f, :, low:high]
                    units.add(m, here, block if len(places) == 2 else beside([block]))
                queue.some(1)
            for m, (f, tile) in enumerate(pair):
                product = units.pop(m, here)
                for i, (slot, block) in enumerate(tile):
                    g = f + slot
                    lanes = blocks[block]
                    term = product[:, i * LANES : (i + 1) * LANES]
                    if f > 0 and slot < 2:
                        term = term + facc[g, :, lanes]
                    if slot > 0:
                        facc[g, :, lanes] = term
                        continue
                    base = tail[odd, :, lanes] if g == final else part_ref[g, odd, :, lanes]
                    done_s[g, odd, :, lanes] = (base + far_scale * term).astype(BF16)
        queue.until(len(queue.items))
        copies = []
        for f in range(frames):
            for side in range(2):
                copies.append(pltpu.make_async_copy(
                    done_s.at[f, side], out_hbm.at[f, side * (rows - 1)], o_sem.at[f, side]))
                copies[-1].start()
        inner.wait()
        for copy in copies:
            copy.wait()

    pl.run_scoped(run, *[pltpu.ACC(m)((width, SIDE), F32) for m in range(MXUS) for _ in range(ACCS)])


def per_device(latents, gamma, weight, bias, intersection, ramp):
    frames, rows, width, chans = latents.shape
    deep = TAPS * chans
    gamma = gamma.reshape(1, chans)
    bias = bias.reshape(1, chans)
    weight = weight.reshape(TAPS, TAPS, deep, chans)
    count = lax.axis_size("rows")
    smem = pl.BlockSpec(memory_space=pltpu.SMEM)
    vmem = pl.BlockSpec(memory_space=pltpu.VMEM)
    hbm = pl.BlockSpec(memory_space=pltpu.HBM)
    anywhere = pl.BlockSpec(memory_space=pl.ANY)
    dma = pltpu.SemaphoreType.DMA
    inside = lambda array: pltpu.with_memory_space_constraint(array, pltpu.VMEM)
    outside = lambda array: pltpu.with_memory_space_constraint(array, pltpu.HBM)
    swap = lambda array, start: lax.ppermute(array, "rows", [
        pair for k in range(start, count - 1, 2) for pair in ((k, k + 1), (k + 1, k))])
    halo = pltpu.VMEM((frames, width, chans), BF16)
    far, near = pl.pallas_call(
        select,
        out_shape=(halo, halo),
        in_specs=[hbm],
        out_specs=(vmem, vmem),
        scratch_shapes=[dma((2,))],
        name="select",
    )(outside(latents))
    near = swap(near, 0)
    far = swap(far, 1)
    out, part, weight, last, carry, nacc = pl.pallas_call(
        interior,
        out_shape=(
            jax.ShapeDtypeStruct(latents.shape, BF16),
            pltpu.VMEM((frames - 1, 2, width, chans), F32),
            pltpu.VMEM(weight.shape, BF16),
            pltpu.VMEM((rows, width, deep), BF16),
            pltpu.VMEM((rows, width, chans), F32),
            pltpu.VMEM((frames, width, chans), F32),
        ),
        in_specs=[smem, smem, vmem, vmem, hbm, vmem, vmem],
        out_specs=(anywhere,) + (vmem,) * 5,
        scratch_shapes=[
            pltpu.VMEM((rows + 1, width + 16, chans), F32),
            pltpu.VMEM((frames - 1, rows, width, deep), BF16),
            pltpu.VMEM((frames, width, deep), BF16),
            pltpu.VMEM((frames, rows, width, chans), F32),
            pltpu.VMEM((frames - 1, rows - 2, width, chans), BF16),
            dma((TAPS, TAPS)),
            dma((frames - 1,)),
        ],
        cost_estimate=pl.CostEstimate(
            flops=2 * 84 * width * deep * chans, bytes_accessed=14 * 2**20, transcendentals=0
        ),
        compiler_params=pltpu.CompilerParams(vmem_limit_bytes=24 * 2**20),
        name="interior",
    )(intersection, ramp, inside(latents), inside(near), outside(weight), gamma, bias)
    return pl.pallas_call(
        edges,
        out_shape=jax.ShapeDtypeStruct(latents.shape, BF16),
        in_specs=[smem, smem] + [vmem] * 7 + [anywhere],
        out_specs=anywhere,
        input_output_aliases={9: 0},
        scratch_shapes=[
            pltpu.VMEM((1, width + 16, chans), F32),
            pltpu.VMEM((frames, width, deep), BF16),
            pltpu.VMEM((rows, width, chans), F32),
            pltpu.VMEM((frames, width, chans), F32),
            pltpu.VMEM((2, width, chans), F32),
            pltpu.VMEM((frames, 2, width, chans), BF16),
            pltpu.VMEM((rows - 2, width, chans), BF16),
            dma((frames, 2)),
            dma(()),
        ],
        cost_estimate=pl.CostEstimate(
            flops=2 * 24 * width * deep * chans, bytes_accessed=4 * 2**20, transcendentals=0
        ),
        compiler_params=pltpu.CompilerParams(vmem_limit_bytes=16 * 2**20),
        name="edges",
    )(
        intersection, ramp, inside(far), inside(weight), gamma, inside(part), inside(last),
        inside(carry), inside(nacc), out,
    )


def solution(mesh):
    in_specs = (P("clips", "rows", None, None), P(), P(), P(), P("clips"), P("clips"))
    out_specs = P("clips", "rows", None, None)
    return jax.shard_map(
        per_device, mesh=mesh, in_specs=in_specs, out_specs=out_specs, check_vma=False
    )
```

time: 222 us -> 31.9 us (0.14); the launches traced: 218 us -> 31.7 us
  matrix products: 166 us -> 0 us
  waiting for transfers between devices: 31.5 us -> 0.01 us
  Pallas kernels: 0 us -> 26.8 us
  other arithmetic: 10.7 us -> 0 us
  local copies, waits for them, and re-layouts: 3.76 us -> 0.03 us
    dot_general x27 -> x0, matrix products: 166 us -> none  [convolve(): jnp.einsum('fhwc,cd->fhwd', slab, weight[step_t, step_h, step_w], preferr...]
    ppermute x2, waiting for transfers between devices: 31.5 us -> 0.01 us  [per_device(): lax.ppermute(array, 'rows', [pair for k in range(start, count - 1, 2) for...]
    pallas_call x0 -> x3, Pallas kernels: none -> 26.8 us  [the longest x1 19.8 us: per_device(): pl.pallas_call(interior, out_shape=(jax.ShapeDtypeStruct(latents.shape, B...]
    convert_element_type x3 -> x0, other arithmetic: 5.71 us -> none  [the longest x1 4.05 us: activate(): return (jax.nn.silu(normed) * keep).astype(jnp.bfloat16)]
    reduce_sum x1 -> x0, other arithmetic: 2.8 us -> none  [activate(): square = jnp.mean(values * values, axis=-1, keepdims=True)]
  transfers between devices with their start and end apart: 2 -> 2, of which waited for: 2 -> 0; matrix products, arithmetic and copies ran while one was open for 1% -> 0% of each run, Pallas kernels for 0% -> 62%
where the time goes in v2:
time: 31.9 us; the launch traced here: 31.7 us
  Pallas kernels  26.8 us (84%)
  starting transfers between devices  4.62 us (14%)
    pallas_call x1, Pallas kernels, per_device(): pl.pallas_call(interior, out_shape=(jax.ShapeDtypeStruct(latents.shape, B...  19.8 us
    pallas_call x1, Pallas kernels, per_device(): pl.pallas_call(edges, out_shape=jax.ShapeDtypeStruct(latents.shape, BF16)...  5.67 us
    ppermute x2, starting transfers between devices, per_device(): lax.ppermute(array, 'rows', [pair for k in range(start, count - 1, 2) for...  4.62 us
    pallas_call x1, Pallas kernels, per_device(): pl.pallas_call(select, out_shape=(halo, halo), in_specs=[hbm], out_specs=...  1.34 us
  transfers between devices with their start and end apart: 2, of which 0 were waited for; matrix products, arithmetic and copies ran while one was open for 0% of the time, Pallas kernels for 62%

profile of v2, /device:TPU:1, one launch (start us, length us, event | category | flops | bytes accessed | tf_op | source)
XLA Modules:
  0.0 31.7 jit_solution(1281511971319115818)
XLA Ops:
  0.0 0.0 copy-start
  0.0 0.0 copy-start.3
  0.0 0.0 copy-start.4
  0.0 0.0 copy-start.2
  0.0 0.0 copy-start.1
  0.0 1.3 %select.1 = (bf16[4,160,384]{2,1,0:T(8,128)(2,1)S(1)}, bf16[4,160,384]{2,1,0:T(8,128)(2,1)S(1)}) custom-call(bf16[4,4,160,384]{3,2,1,0:T(8,128)(2,1)} %x_ref.1), custom_call_target="tpu_custom_call" | custom-call | tf_op jit(solution)/shard_map/select/pallas_call | solution.py:466
  1.4 0.1 collective-permute-start.1
  1.5 4.5 %collective-permute-start = (bf16[4,160,384]{2,1,0:T(8,128)(2,1)S(1)}, bf16[4,160,384]{2,1,0:T(8,128)(2,1)S(1)}, u32[]{:S(2)}, u32[]{:S(2)}) collective-permute-start(bf16[4,160,384]{2,1,0:T(8,128)(2,1)S(1)} %get-tuple-element.13), channel_id=1, source_target_pairs={{1,2},{2,1},{3,4},{4,3},{5,6},{6,5},{7,8},{8,7},{9,10},{10,9},{11,... | collective-permute-start | bytes 1474568 | tf_op jit(solution)/shard_map/ppermute | solution.py:463
  6.0 0.0 copy-done.3
  6.0 0.0 copy-done.4
  6.0 0.0 collective-permute-done.1.near_ref
  6.1 0.0 copy-done
  6.1 0.0 copy-done.2
  6.1 0.0 copy-done.1
  6.1 19.8 %interior.1 = (bf16[4,4,160,384]{3,2,1,0:T(8,128)(2,1)}, f32[3,2,160,384]{3,2,1,0:T(8,128)S(1)}, bf16[3,3,1152,384]{3,2,1,0:T(8,128)(2,1)S(1)}, bf16[4,160,1152]...) custom-call(s32[16]{0:T(128)S(1)} %copy-done.1, s32[16]{0:T(128)S(1)} %copy-done.2, ...), custom_call_target="tpu_custom_call" | custom-call | flops 11890851840 | bytes 14680064 | tf_op jit(solution)/shard_map/interior/pallas_call | solution.py:476
  25.9 0.0 collective-permute-done.far_ref
  25.9 5.7 %edges.1 = bf16[4,4,160,384]{3,2,1,0:T(8,128)(2,1)} custom-call(s32[16]{0:T(128)S(1)} %copy-done.1, s32[16]{0:T(128)S(1)} %copy-done.2, bf16[4,160,384]{2,1,0:T(8,128)(2,1)S(1)} %collective-permute-done.far_ref, bf16[3,3,1152,384]{3,2,1,0:T(8,128)(2,1)S(1)} %get-tuple-element.15.w_ref, ...), custom_call_target="tpu_custom_call", output_to_operand_aliasing={{}: (9, {})} | custom-call | flops 3397386240 | bytes 4194304 | tf_op jit(solution)/shard_map/edges/pallas_call | solution.py:503
  (2 shorter events, 0.0 us)
Async XLA Ops:
  0.0 6.1 %copy-start = (bf16[4,4,160,384]{3,2,1,0:T(8,128)(2,1)S(1)}, bf16[4,4,160,384]{3,2,1,0:T(8,128)(2,1)}, u32[]{:S(2)}) copy-start(bf16[4,4,160,384]{3,2,1,0:T(8,128)(2,1)} %x_ref.1) | copy-start | bytes 5898244
  0.0 6.0 %copy-start.3 = (f32[384]{0:T(512)S(1)}, f32[384]{0:T(512)}, u32[]{:S(2)}) copy-start(f32[384]{0:T(512)} %param.7) | copy-start | bytes 4612
  0.0 6.0 %copy-start.4 = (f32[384]{0:T(512)S(1)}, f32[384]{0:T(512)}, u32[]{:S(2)}) copy-start(f32[384]{0:T(512)} %param.9) | copy-start | bytes 4612
  0.0 6.1 %copy-start.2 = (s32[16]{0:T(128)S(1)}, s32[16]{0:T(128)}, u32[]{:S(2)}) copy-start(s32[16]{0:T(128)} %ramp_ref.3) | copy-start | bytes 196
  0.0 6.1 %copy-start.1 = (s32[16]{0:T(128)S(1)}, s32[16]{0:T(128)}, u32[]{:S(2)}) copy-start(s32[16]{0:T(128)} %inter_ref.3) | copy-start | bytes 196
  1.4 4.7 %collective-permute-start.1 = (bf16[4,160,384]{2,1,0:T(8,128)(2,1)S(1)}, bf16[4,160,384]{2,1,0:T(8,128)(2,1)S(1)}, u32[]{:S(2)}, u32[]{:S(2)}) collective-permute-start(bf16[4,160,384]{2,1,0:T(8,128)(2,1)S(1)} %get-tuple-element.14), channel_id=1, source_target_pairs={{0,1},{1,0},{2,3},{3,2},{4,5},{5,4},{6,7},{7,6},{8,9},{9,8},{10,11... | collective-permute-start | bytes 1474568 | tf_op jit(solution)/shard_map/ppermute | solution.py:463
  1.5 24.4 %collective-permute-start = (bf16[4,160,384]{2,1,0:T(8,128)(2,1)S(1)}, bf16[4,160,384]{2,1,0:T(8,128)(2,1)S(1)}, u32[]{:S(2)}, u32[]{:S(2)}) collective-permute-start(bf16[4,160,384]{2,1,0:T(8,128)(2,1)S(1)} %get-tuple-element.13), channel_id=1, source_target_pairs={{1,2},{2,1},{3,4},{4,3},{5,6},{6,5},{7,8},{8,7},{9,10},{10,9},{11,... | collective-permute-start | bytes 1474568 | tf_op jit(solution)/shard_map/ppermute | solution.py:463

commit v3 on v2

--- a/solution.py
+++ b/solution.py
@@ -35,10 +35,9 @@
     return lax.rem(lax.axis_index("rows"), 2)
 
 
-def activate(values, gamma):
+def activate(values, half_gamma):
     square = jnp.mean(values * values, axis=-1, keepdims=True)
-    normed = values * lax.rsqrt(square + 1e-06) * gamma
-    half = 0.5 * normed
+    half = values * lax.rsqrt(square + 1e-06) * half_gamma
     return half + half * jnp.tanh(half)
 
 
@@ -210,26 +209,16 @@
 
 
 def interior(
-    inter_ref, ramp_ref, x_ref, near_ref, w_hbm, gamma_ref, bias_ref,
-    out_hbm, part_ref, w_ref, last_ref, carry_ref, nacc_ref,
-    line, flat, nflat, acc, done_s, w_sem, o_sem,
+    inter_ref, ramp_ref, x_ref, near_ref, w_ref, gamma_ref, bias_ref,
+    out_hbm, part_ref, last_ref, carry_ref, nacc_ref,
+    line, flat, nflat, acc, done_s, o_sem,
 ):
     frames, rows, width, chans = x_ref.shape
     depth = TAPS * chans // LANES
     passes = conv_passes(depth)
-    order = [(slot, kh) for slots in ((0, 1), (2,)) for kh in range(TAPS) for slot in slots]
-    w_in = {
-        (slot, kh): pltpu.make_async_copy(
-            w_hbm.at[TAPS - 1 - slot, kh], w_ref.at[TAPS - 1 - slot, kh], w_sem.at[slot, kh])
-        for slot, kh in order
-    }
-    starts = [w_in[key].start for key in order]
-    for start in starts[:4]:
-        start()
-    starts = starts[4:]
     _, below_first, below_second, _ = scales(inter_ref, ramp_ref)
     below = (below_first, below_second)
-    gamma = gamma_ref[...]
+    gamma = 0.5 * gamma_ref[...]
     clear_ends(line)
     near_kh = 2 * (1 - parity())
 
@@ -245,11 +234,6 @@
         ready[f] = queue.add(prepare(near_ref.at[f], gamma, line.at[rows], nflat.at[f]))
 
     def weight(tile, places):
-        for slot, _ in tile:
-            for kh, _ in places:
-                copy = w_in.pop((slot, kh), None)
-                if copy is not None:
-                    copy.wait()
         return cells(w_ref, tile, places)
 
     def contribute(g, r, lanes, term, first, final):
@@ -301,32 +285,17 @@
                             term = term + nacc_ref[f + slot, :, lanes]
                         nacc_ref[f + slot, :, lanes] = term
 
-        queue.until(ready[0, 3] if rows == 4 else ready[0, 0])
-        for start in starts[:3]:
-            start()
-        queue.until(ready[0, 2] if rows == 4 else ready[0, 0])
-        for start in starts[3:]:
-            start()
+        queue.until(ready[0, 0])
         for f in range(frames - 1):
             jobs = jobs_of(tiles_of(chans, min(TAPS, frames - f)), rows)
             for place, job in enumerate(jobs):
                 flat_row = lambda h: flat.at[f, h]
-                if f == 0 and place == 0:
-                    for r in reversed(range(rows)):
-                        queue.until(ready[0, max(r - 1, 0)])
-                        matrix_job(
-                            units, [(tile, [r]) for tile, _ in job], passes, rows, flat_row,
-                            weight, lambda: queue.some(1),
-                            lambda *rest: pop(f, *rest))
-                    near(f, job)
-                    near_pop(f, job)
-                else:
-                    queue.until(ready[f])
-                    matrix_job(
-                        units, job, passes, rows, flat_row, weight,
-                        lambda: queue.some(2), lambda *rest: pop(f, *rest),
-                        lambda: near(f, job))
-                    near_pop(f, job)
+                queue.until(ready[f] if f else 0)
+                matrix_job(
+                    units, job, passes, rows, flat_row, weight,
+                    lambda: queue.some(2), lambda *rest: pop(f, *rest),
+                    lambda: near(f, job))
+                near_pop(f, job)
             copy = pltpu.make_async_copy(
                 done_s.at[f], out_hbm.at[f, pl.ds(1, rows - 2)], o_sem.at[f])
             copy.start()
@@ -359,7 +328,7 @@
     below = (below_first, below_second)
     far_scale = jnp.where(odd == 1, bottom, top)
     near_scale = jnp.where(odd == 1, top, bottom)
-    gamma = gamma_ref[...]
+    gamma = 0.5 * gamma_ref[...]
     clear_ends(line)
     final = frames - 1
     blocks = [slice(b * LANES, (b + 1) * LANES) for b in range(chans // LANES)]
@@ -403,8 +372,9 @@
         inner = pltpu.make_async_copy(
             inner_s, out_hbm.at[final, pl.ds(1, rows - 2)], i_sem)
         inner.start()
+        nears, copies = [], []
         for g in range(frames):
-            queue.add([lambda g=g, at=at: near_row(g, at) for at in range(0, width, CHUNK)])
+            nears.append(queue.add([lambda g=g, at=at: near_row(g, at) for at in range(0, width, CHUNK)]))
         whole = [
             (f, tile) for f in range(frames) for tile in tiles_of(chans, min(TAPS, frames - f))
         ]
@@ -432,13 +402,13 @@
                         continue
                     base = tail[odd, :, lanes] if g == final else part_ref[g, odd, :, lanes]
                     done_s[g, odd, :, lanes] = (base + far_scale * term).astype(BF16)
-        queue.until(len(queue.items))
-        copies = []
-        for f in range(frames):
-            for side in range(2):
-                copies.append(pltpu.make_async_copy(
-                    done_s.at[f, side], out_hbm.at[f, side * (rows - 1)], o_sem.at[f, side]))
-                copies[-1].start()
+                    if block == len(blocks) - 1:
+                        queue.until(nears[g])
+                        for side in range(2):
+                            copies.append(pltpu.make_async_copy(
+                                done_s.at[g, side], out_hbm.at[g, side * (rows - 1)],
+                                o_sem.at[g, side]))
+                            copies[-1].start()
         inner.wait()
         for copy in copies:
             copy.wait()
@@ -469,29 +439,30 @@
         in_specs=[hbm],
         out_specs=(vmem, vmem),
         scratch_shapes=[dma((2,))],
+        cost_estimate=pl.CostEstimate(flops=20 * 10**9, bytes_accessed=4 * 2**20, transcendentals=0),
+        compiler_params=pltpu.CompilerParams(vmem_limit_bytes=2**20),
         name="select",
     )(outside(latents))
+    weight = inside(weight)
     near = swap(near, 0)
     far = swap(far, 1)
-    out, part, weight, last, carry, nacc = pl.pallas_call(
+    out, part, last, carry, nacc = pl.pallas_call(
         interior,
         out_shape=(
             jax.ShapeDtypeStruct(latents.shape, BF16),
             pltpu.VMEM((frames - 1, 2, width, chans), F32),
-            pltpu.VMEM(weight.shape, BF16),
             pltpu.VMEM((rows, width, deep), BF16),
             pltpu.VMEM((rows, width, chans), F32),
             pltpu.VMEM((frames, width, chans), F32),
         ),
-        in_specs=[smem, smem, vmem, vmem, hbm, vmem, vmem],
-        out_specs=(anywhere,) + (vmem,) * 5,
+        in_specs=[smem, smem, vmem, vmem, vmem, vmem, vmem],
+        out_specs=(anywhere,) + (vmem,) * 4,
         scratch_shapes=[
             pltpu.VMEM((rows + 1, width + 16, chans), F32),
             pltpu.VMEM((frames - 1, rows, width, deep), BF16),
             pltpu.VMEM((frames, width, deep), BF16),
             pltpu.VMEM((frames, rows, width, chans), F32),
             pltpu.VMEM((frames - 1, rows - 2, width, chans), BF16),
-            dma((TAPS, TAPS)),
             dma((frames - 1,)),
         ],
         cost_estimate=pl.CostEstimate(
@@ -499,7 +470,7 @@
         ),
         compiler_params=pltpu.CompilerParams(vmem_limit_bytes=24 * 2**20),
         name="interior",
-    )(intersection, ramp, inside(latents), inside(near), outside(weight), gamma, bias)
+    )(intersection, ramp, inside(latents), inside(near), weight, gamma, bias)
     return pl.pallas_call(
         edges,
         out_shape=jax.ShapeDtypeStruct(latents.shape, BF16),
@@ -523,7 +494,7 @@
         compiler_params=pltpu.CompilerParams(vmem_limit_bytes=16 * 2**20),
         name="edges",
     )(
-        intersection, ramp, inside(far), inside(weight), gamma, inside(part), inside(last),
+        intersection, ramp, inside(far), weight, gamma, inside(part), inside(last),
         inside(carry), inside(nacc), out,
     )
 

time: 31.9 us -> 29 us (0.909)
  Pallas kernels: 26.8 us -> 23.7 us
    pallas_call x1, Pallas kernels: 19.8 us -> 17 us  [per_device(): pl.pallas_call(interior, out_shape=(jax.ShapeDtypeStruct(latents.shape, B...]
    pallas_call x1, Pallas kernels: 5.67 us -> 5.28 us  [per_device(): pl.pallas_call(edges, out_shape=jax.ShapeDtypeStruct(latents.shape, BF16)...]
  transfers between devices with their start and end apart: 2 -> 2, of which waited for: 0 -> 0; matrix products, arithmetic and copies ran while one was open for 0% -> 0% of each run, Pallas kernels for 62% -> 59%
where the time goes in v3:
time: 29 us; the launch traced here: 28.9 us
  Pallas kernels  23.7 us (82%)
  starting transfers between devices  4.88 us (17%)
  between operations  0.29 us (1%)
    pallas_call x1, Pallas kernels, per_device(): pl.pallas_call(interior, out_shape=(jax.ShapeDtypeStruct(latents.shape, B...  17 us
    pallas_call x1, Pallas kernels, per_device(): pl.pallas_call(edges, out_shape=jax.ShapeDtypeStruct(latents.shape, BF16)...  5.28 us
    ppermute x2, starting transfers between devices, per_device(): lax.ppermute(array, 'rows', [pair for k in range(start, count - 1, 2) for...  4.88 us
    pallas_call x1, Pallas kernels, per_device(): pl.pallas_call(select, out_shape=(halo, halo), in_specs=[hbm], out_specs=...  1.36 us
  transfers between devices with their start and end apart: 2, of which 0 were waited for; matrix products, arithmetic and copies ran while one was open for 0% of the time, Pallas kernels for 59%

profile of v3, /device:TPU:1, one launch (start us, length us, event | category | flops | bytes accessed | tf_op | source)
XLA Modules:
  0.0 28.9 jit_solution(7409686570448305484)
XLA Ops:
  0.0 0.0 copy-start.3
  0.0 0.0 copy-start.4
  0.0 0.0 copy-start.5
  0.0 0.0 copy-start.2
  0.0 0.0 copy-start.1
  0.0 0.0 copy-start
  0.0 1.4 %select.1 = (bf16[4,160,384]{2,1,0:T(8,128)(2,1)S(1)}, bf16[4,160,384]{2,1,0:T(8,128)(2,1)S(1)}) custom-call(bf16[4,4,160,384]{3,2,1,0:T(8,128)(2,1)} %x_ref.1), custom_call_target="tpu_custom_call" | custom-call | flops 20000000000 | bytes 4194304 | tf_op jit(solution)/shard_map/select/pallas_call | solution.py:436
  1.4 0.1 collective-permute-start.1
  1.5 4.8 %collective-permute-start = (bf16[4,160,384]{2,1,0:T(8,128)(2,1)S(1)}, bf16[4,160,384]{2,1,0:T(8,128)(2,1)S(1)}, u32[]{:S(2)}, u32[]{:S(2)}) collective-permute-start(bf16[4,160,384]{2,1,0:T(8,128)(2,1)S(1)} %get-tuple-element.12), channel_id=1, source_target_pairs={{1,2},{2,1},{3,4},{4,3},{5,6},{6,5},{7,8},{8,7},{9,10},{10,9},{11,... | collective-permute-start | bytes 1474568 | tf_op jit(solution)/shard_map/ppermute | solution.py:433
  6.3 0.0 copy-done.4
  6.3 0.0 copy-done.5
  6.3 0.0 collective-permute-done.1.near_ref
  6.3 0.0 copy-done.3
  6.4 0.0 copy-done.2
  6.4 0.0 copy-done.1
  6.4 0.0 copy-done
  6.4 17.0 %interior.1 = (bf16[4,4,160,384]{3,2,1,0:T(8,128)(2,1)}, f32[3,2,160,384]{3,2,1,0:T(8,128)S(1)}, bf16[4,160,1152]{2,1,0:T(8,128)(2,1)S(1)}, f32[4,160,384]{2,1,0:T(8,128)S(1)}, f32[4,160,384]{2,1,0:T(8,128)S(1)}) custom-call(s32[16]{0:T(128)S(1)} %copy-done.1, s32[16]{0:T(128)S(1)} %copy-done.2, bf16[4,4,160,384]{3,2,1,0:T(8,128)(2,1)S(1)} %copy-done.3, ...), custom_call_target="tpu_custom_call" | custom-call | flops 11890851840 | bytes 14680064 | tf_op jit(solution)/shard_map/interior/pallas_call | solution.py:449
  23.4 0.0 collective-permute-done.far_ref
  23.4 5.3 %edges.1 = bf16[4,4,160,384]{3,2,1,0:T(8,128)(2,1)} custom-call(s32[16]{0:T(128)S(1)} %copy-done.1, s32[16]{0:T(128)S(1)} %copy-done.2, bf16[4,160,384]{2,1,0:T(8,128)(2,1)S(1)} %collective-permute-done.far_ref, bf16[3,3,1152,384]{3,2,1,0:T(8,128)(2,1)S(1)} %bitcast.2, f32[1,384]{1,0:T(1,128)S(1)} %reshape.10.gamma_ref, ...), custom_call_target="tpu_custom_call", output_to_operand_aliasing={{}: (9, {})} | custom-call | flops 3397386240 | bytes 4194304 | tf_op jit(solution)/shard_map/edges/pallas_call | solution.py:474
  (2 shorter events, 0.0 us)
Async XLA Ops:
  0.0 6.3 %copy-start.3 = (bf16[4,4,160,384]{3,2,1,0:T(8,128)(2,1)S(1)}, bf16[4,4,160,384]{3,2,1,0:T(8,128)(2,1)}, u32[]{:S(2)}) copy-start(bf16[4,4,160,384]{3,2,1,0:T(8,128)(2,1)} %x_ref.1) | copy-start | bytes 5898244
  0.0 6.3 %copy-start.4 = (f32[384]{0:T(512)S(1)}, f32[384]{0:T(512)}, u32[]{:S(2)}) copy-start(f32[384]{0:T(512)} %param.7) | copy-start | bytes 4612
  0.0 6.3 %copy-start.5 = (f32[384]{0:T(512)S(1)}, f32[384]{0:T(512)}, u32[]{:S(2)}) copy-start(f32[384]{0:T(512)} %param.9) | copy-start | bytes 4612
  0.0 6.3 %copy-start.2 = (s32[16]{0:T(128)S(1)}, s32[16]{0:T(128)}, u32[]{:S(2)}) copy-start(s32[16]{0:T(128)} %ramp_ref.3) | copy-start | bytes 196
  0.0 6.3 %copy-start.1 = (s32[16]{0:T(128)S(1)}, s32[16]{0:T(128)}, u32[]{:S(2)}) copy-start(s32[16]{0:T(128)} %inter_ref.3) | copy-start | bytes 196
  0.0 6.3 %copy-start = (bf16[3,3,3,384,384]{4,3,2,1,0:T(8,128)(2,1)S(1)}, bf16[3,3,3,384,384]{4,3,2,1,0:T(8,128)(2,1)}, u32[]{:S(2)}) copy-start(bf16[3,3,3,384,384]{4,3,2,1,0:T(8,128)(2,1)} %param.8) | copy-start | bytes 23887876
  1.4 4.9 %collective-permute-start.1 = (bf16[4,160,384]{2,1,0:T(8,128)(2,1)S(1)}, bf16[4,160,384]{2,1,0:T(8,128)(2,1)S(1)}, u32[]{:S(2)}, u32[]{:S(2)}) collective-permute-start(bf16[4,160,384]{2,1,0:T(8,128)(2,1)S(1)} %get-tuple-element.13), channel_id=1, source_target_pairs={{0,1},{1,0},{2,3},{3,2},{4,5},{5,4},{6,7},{7,6},{8,9},{9,8},{10,11... | collective-permute-start | bytes 1474568 | tf_op jit(solution)/shard_map/ppermute | solution.py:433
  1.5 21.9 %collective-permute-start = (bf16[4,160,384]{2,1,0:T(8,128)(2,1)S(1)}, bf16[4,160,384]{2,1,0:T(8,128)(2,1)S(1)}, u32[]{:S(2)}, u32[]{:S(2)}) collective-permute-start(bf16[4,160,384]{2,1,0:T(8,128)(2,1)S(1)} %get-tuple-element.12), channel_id=1, source_target_pairs={{1,2},{2,1},{3,4},{4,3},{5,6},{6,5},{7,8},{8,7},{9,10},{10,9},{11,... | collective-permute-start | bytes 1474568 | tf_op jit(solution)/shard_map/ppermute | solution.py:433

commit v4 on v3

--- a/solution.py
+++ b/solution.py
@@ -10,7 +10,8 @@
 TAPS = 3
 LANES = 128
 SIDE = 256
-CHUNK = 32
+RATE = 0.3
+CHUNK = 80
 MXUS = 2
 ACCS = 6
 
@@ -46,13 +47,16 @@
 
     def first(at):
         act = activate(source[at : at + CHUNK].astype(F32), gamma)
-        line[8 + at : 8 + at + CHUNK] = act
+        for block in range(chans // LANES):
+            line[block, 8 + at : 8 + at + CHUNK] = act[:, block * LANES : (block + 1) * LANES]
         target[at : at + CHUNK, chans : 2 * chans] = act.astype(BF16)
 
     def second(at):
         for step in (0, 2):
-            piece = line[7 + step + at : 7 + step + at + CHUNK]
-            target[at : at + CHUNK, step * chans : (step + 1) * chans] = piece.astype(BF16)
+            for block in range(chans // LANES):
+                piece = line[block, 7 + step + at : 7 + step + at + CHUNK]
+                low = step * chans + block * LANES
+                target[at : at + CHUNK, low : low + LANES] = piece.astype(BF16)
 
     for at in range(0, width, CHUNK):
         yield lambda at=at: first(at)
@@ -61,15 +65,16 @@
 
 
 def clear_ends(line):
-    lines, padded, chans = line.shape
-    line[:, 0:8] = jnp.zeros((lines, 8, chans), F32)
-    line[:, padded - 8 : padded] = jnp.zeros((lines, 8, chans), F32)
+    lines, blocks, padded, lanes = line.shape
+    line[:, :, 0:8] = jnp.zeros((lines, blocks, 8, lanes), F32)
+    line[:, :, padded - 8 : padded] = jnp.zeros((lines, blocks, 8, lanes), F32)
 
 
 class Queue:
     def __init__(self):
         self.items = []
         self.done = 0
+        self.credit = 0.0
 
     def add(self, steps):
         self.items.extend(steps)
@@ -81,7 +86,10 @@
             self.done += 1
 
     def some(self, number):
-        self.until(min(len(self.items), self.done + number))
+        self.credit += number
+        whole = int(self.credit)
+        self.credit -= whole
+        self.until(min(len(self.items), self.done + whole))
 
 
 def tiles_of(chans, count):
@@ -94,7 +102,7 @@
     jobs = [
         [(tiles[i], full), (tiles[i + 1], full)] for i in range(0, len(tiles) - 1, 2)
     ]
-    if len(tiles) % 2:
+    if len(tiles) % 2 and len(tiles[-1]) > 1:
         jobs.append([(tiles[-1], full[: rows // 2]), (tiles[-1], full[rows // 2 :])])
     return jobs
 
@@ -182,6 +190,7 @@
                 for m, _, rows_of in active:
                     if r in rows_of:
                         units.add(m, acc_of(r, places, rows), block)
+                step()
         if between is not None and number == len(passes) - 3:
             between()
         for r in (3, 1, 0, 2):
@@ -192,7 +201,71 @@
                 for m, (tile, rows_of) in enumerate(job):
                     if r in rows_of:
                         pop(m, tile, here, r, last)
-        step()
+
+
+def crossed(w_ref, slot, block, khs, chunks):
+    columns = []
+    for kh in khs:
+        parts = [
+            w_ref[TAPS - 1 - slot, kh, rest * LANES : (rest + 1) * LANES,
+                  block * LANES : (block + 1) * LANES]
+            for rest in chunks
+        ]
+        while len(parts) < 2:
+            parts.append(jnp.zeros((LANES, LANES), BF16))
+        columns.append(jnp.concatenate(parts, axis=0))
+    return jnp.concatenate(columns, axis=1)
+
+
+def crossed_terms(rows):
+    middle = rows // 2
+    upper = [
+        (h, [(0, h + 1, 0)] + ([(1, h, 1)] if h < middle else [])) for h in range(rows - 1)
+    ]
+    lower = [
+        (h, [(0, h - 1, 2)] + ([(1, h, 1)] if h >= middle else [])) for h in range(1, rows)
+    ]
+    return upper, lower
+
+
+def crossed_steps(units, m, part, numbers, w_ref, slot, block, depth, rows, flat_row):
+    khs = ((0, 1), (2, 1))[part]
+    heights = [h for h, _ in crossed_terms(rows)[part]]
+    for chunks in in_pairs(range(depth)):
+        yield 0, lambda chunks=chunks: units.weights(
+            m, crossed(w_ref, slot, block, khs, chunks))
+        for h in heights:
+            yield 1, lambda chunks=chunks, h=h: units.add(m, numbers[h], beside(
+                [flat_row(h)[:, c * LANES : (c + 1) * LANES] for c in chunks]))
+
+
+def crossed_pops(units, places, rows, give):
+    items = []
+    for part, (m, numbers) in enumerate(places):
+        for h, uses in crossed_terms(rows)[part]:
+            items.append((m, numbers[h], uses))
+    order = [r for _, _, uses in items for _, r, _ in uses]
+    seen = 0
+    for m, number, uses in items:
+        product = units.pop(m, number)
+        for half, r, kh in uses:
+            term = product[:, half * LANES : (half + 1) * LANES]
+            give(r, kh, term, r not in order[:seen], r not in order[seen + 1 :])
+            seen += 1
+
+
+def merged(streams, step):
+    streams = [list(stream) for stream in streams]
+    totals = [max(1, sum(cost for cost, _ in stream)) for stream in streams]
+    spent = [0] * len(streams)
+    while any(streams):
+        live = [i for i, stream in enumerate(streams) if stream]
+        i = min(live, key=lambda i: spent[i] / totals[i])
+        cost, run = streams[i].pop(0)
+        run()
+        spent[i] += cost
+        if cost:
+            step()
 
 
 def select(x_hbm, far_ref, near_ref, sem):
@@ -210,7 +283,7 @@
 
 def interior(
     inter_ref, ramp_ref, x_ref, near_ref, w_ref, gamma_ref, bias_ref,
-    out_hbm, part_ref, last_ref, carry_ref, nacc_ref,
+    out_hbm, part_ref, last_ref, carry_ref, nacc_ref, late_ref,
     line, flat, nflat, acc, done_s, o_sem,
 ):
     frames, rows, width, chans = x_ref.shape
@@ -237,16 +310,20 @@
         return cells(w_ref, tile, places)
 
     def contribute(g, r, lanes, term, first, final):
+        total, at = (carry_ref, (r,)) if g == frames - 1 else (acc, (g, r))
+        at = at + (slice(None), lanes)
         if first:
             term = term + (x_ref[g, r, :, lanes].astype(F32) + bias_ref[:, lanes])
         else:
-            term = term + acc[g, r, :, lanes]
+            term = term + total[at]
         if not final:
-            acc[g, r, :, lanes] = term
+            total[at] = term
         elif r == 0:
             part_ref[g, 0, :, lanes] = term
         elif r == rows - 1:
             part_ref[g, 1, :, lanes] = term
+        elif g == frames - 2:
+            late_ref[r - 1, :, lanes] = term.astype(BF16)
         else:
             done_s[g, r - 1, :, lanes] = term.astype(BF16)
 
@@ -264,60 +341,84 @@
                     f + slot, r, lanes, term,
                     (f == 0 or slot == 2) and number < 4, slot == 0 and last)
 
-        def near(f, job):
-            queue.until(ready[f])
+        whole = [
+            (f, tile) for f in range(frames) for tile in tiles_of(chans, min(TAPS, frames - f))
+        ]
+        slots = in_pairs(whole)
+
+        def near(slot_pair, number=0):
+            for f, _ in slot_pair:
+                queue.until(ready[f])
             for places in in_pairs([(near_kh, c) for c in range(depth)]):
                 low, high = places[0][1] * LANES, (places[-1][1] + 1) * LANES
-                for m, (tile, _) in enumerate(job):
-                    if m == 0 or tile is not job[0][0]:
-                        units.weights(m, cells(w_ref, tile, places))
-                        block = nflat[f, :, low:high]
-                        units.add(m, 0, block if len(places) == 2 else beside([block]))
-
-        def near_pop(f, job):
-            for m, (tile, _) in enumerate(job):
-                if m == 0 or tile is not job[0][0]:
-                    product = units.pop(m, 0)
-                    for i, (slot, block) in enumerate(tile):
-                        lanes = slice(block * LANES, (block + 1) * LANES)
-                        term = product[:, i * LANES : (i + 1) * LANES]
-                        if f > 0 and slot < 2:
-                            term = term + nacc_ref[f + slot, :, lanes]
-                        nacc_ref[f + slot, :, lanes] = term
+                for m, (f, tile) in enumerate(slot_pair):
+                    units.weights(m, cells(w_ref, tile, places))
+                for m, (f, tile) in enumerate(slot_pair):
+                    block = nflat[f, :, low:high]
+                    units.add(m, number, block if len(places) == 2 else beside([block]))
+
+        def near_pop(slot_pair, number=0):
+            for m, (f, tile) in enumerate(slot_pair):
+                product = units.pop(m, number)
+                for i, (slot, block) in enumerate(tile):
+                    lanes = slice(block * LANES, (block + 1) * LANES)
+                    term = product[:, i * LANES : (i + 1) * LANES]
+                    if f > 0 and slot < 2:
+                        term = term + nacc_ref[f + slot, :, lanes]
+                    nacc_ref[f + slot, :, lanes] = term
 
         queue.until(ready[0, 0])
+        copies = []
         for f in range(frames - 1):
             jobs = jobs_of(tiles_of(chans, min(TAPS, frames - f)), rows)
             for place, job in enumerate(jobs):
                 flat_row = lambda h: flat.at[f, h]
-                queue.until(ready[f] if f else 0)
+                if f:
+                    queue.until(ready[f, 0])
+                here = slots.pop(0)
                 matrix_job(
                     units, job, passes, rows, flat_row, weight,
-                    lambda: queue.some(2), lambda *rest: pop(f, *rest),
-                    lambda: near(f, job))
-                near_pop(f, job)
-            copy = pltpu.make_async_copy(
-                done_s.at[f], out_hbm.at[f, pl.ds(1, rows - 2)], o_sem.at[f])
-            copy.start()
-        f = frames - 1
-        queue.until(ready[f])
-        tiles = tiles_of(chans, 1)
-        job = [(tile, None) for tile in tiles]
-        near(f, job)
-        near_pop(f, job)
-        for r in range(rows):
-            carry_ref[r] = acc[f, r]
-        for f in range(frames - 1):
-            pltpu.make_async_copy(
-                done_s.at[f], out_hbm.at[f, pl.ds(1, rows - 2)], o_sem.at[f]).wait()
+                    lambda: queue.some(RATE), lambda *rest: pop(f, *rest),
+                    lambda: near(here))
+                near_pop(here)
+            tile = tiles_of(chans, min(TAPS, frames - f))[-1]
+            if len(tile) == 1:
+                (slot, block), here = tile[0], slots.pop(0)
+                numbers = {h: h for h in range(rows)}
+                flat_row = lambda h: flat.at[f, h]
+                merged([
+                    crossed_steps(
+                        units, part, part, numbers, w_ref, slot, block, depth, rows, flat_row)
+                    for part in range(MXUS)
+                ], lambda: queue.some(RATE))
+                near(here, 4)
+
+                def give(r, kh, term, first, last):
+                    if kh == 2 and r < 2:
+                        term = term * below[r]
+                    contribute(
+                        f + slot, r, slice(block * LANES, (block + 1) * LANES), term,
+                        first and (f == 0 or slot == 2), last and slot == 0)
+
+                crossed_pops(units, [(0, numbers), (1, numbers)], rows, give)
+                near_pop(here, 4)
+            if f < frames - 2:
+                copies.append(pltpu.make_async_copy(
+                    done_s.at[f], out_hbm.at[f, pl.ds(1, rows - 2)], o_sem.at[f]))
+                copies[-1].start()
+        for here in slots:
+            near(here)
+            near_pop(here)
+        for copy in copies:
+            copy.wait()
 
     pl.run_scoped(run, *[pltpu.ACC(m)((width, SIDE), F32) for m in range(MXUS) for _ in range(ACCS)])
 
 
 def edges(
-    inter_ref, ramp_ref, far_ref, w_ref, gamma_ref, part_ref, last_ref, carry_ref, nacc_ref, _,
+    inter_ref, ramp_ref, far_ref, w_ref, gamma_ref, part_ref, last_ref, carry_ref, nacc_ref, late_ref, _,
     out_hbm,
-    line, fflat, acc, facc, tail, done_s, inner_s, o_sem, i_sem,
+    line, fflat, acc, facc, tail, done_s, inner_s, o_sem, i_sem, l_sem,
 ):
     frames, width, chans = far_ref.shape
     rows = out_hbm.shape[1]
@@ -331,6 +432,8 @@
     gamma = 0.5 * gamma_ref[...]
     clear_ends(line)
     final = frames - 1
+    late = pltpu.make_async_copy(late_ref, out_hbm.at[final - 1, pl.ds(1, rows - 2)], l_sem)
+    late.start()
     blocks = [slice(b * LANES, (b + 1) * LANES) for b in range(chans // LANES)]
 
     queue = Queue()
@@ -348,27 +451,55 @@
     def run(*accs):
         units = Units(accs)
 
-        def pop(m, tile, number, r, last):
+        def contribute(r, lanes, term, first, last):
+            term = term + (carry_ref if first else acc)[r, :, lanes]
+            if not last:
+                acc[r, :, lanes] = term
+            elif r == 0 or r == rows - 1:
+                tail[0 if r == 0 else 1, :, lanes] = term
+            else:
+                inner_s[r - 1, :, lanes] = term.astype(BF16)
+
+        def pop(m, tile, number, r, kept, last):
             product = units.pop(m, number)
             for i, (_, block) in enumerate(tile):
-                lanes = blocks[block]
                 term = product[:, i * LANES : (i + 1) * LANES]
-                if number >= 4:
-                    term = acc[r, :, lanes] + term * below[r]
-                else:
-                    term = carry_ref[r, :, lanes] + term
-                if not last:
-                    acc[r, :, lanes] = term
-                elif r == 0 or r == rows - 1:
-                    tail[0 if r == 0 else 1, :, lanes] = term
-                else:
-                    inner_s[r - 1, :, lanes] = term.astype(BF16)
-
-        tiles = tiles_of(chans, 1)
-        job = [(tile, range(rows)) for tile in tiles]
-        matrix_job(
-            units, job, passes, rows, lambda h: last_ref.at[h],
-            lambda tile, places: cells(w_ref, tile, places), lambda: queue.some(2), pop)
+                contribute(r, blocks[block], term * below[r] if kept else term, not kept, last)
+
+        def taps(m, tile, rows_of, numbers):
+            for number, places in enumerate(passes):
+                active = [r for r in rows_of if acc_of(r, places, rows) is not None]
+                if active:
+                    yield 0, lambda places=places: units.weights(m, cells(w_ref, tile, places))
+                for r in active:
+                    yield 1, lambda r=r, places=places: units.add(
+                        m, numbers[acc_of(r, places, rows)], row_block(flat_row, r, places))
+                for r in active:
+                    here = acc_of(r, places, rows)
+                    later = [acc_of(r, other, rows) for other in passes[number + 1 :]]
+                    if here not in later:
+                        yield 0, lambda r=r, here=here, last=all(o is None for o in later): pop(
+                            m, tile, numbers[here], r, here >= rows, last)
+
+        flat_row = lambda h: last_ref.at[h]
+        first_tile, rest = tiles_of(chans, 1)
+        (_, block), = rest
+        upper = {h: h for h in range(rows)}
+        lower = {h: 2 + h for h in range(rows)}
+
+        def give(r, kh, term, first, last):
+            contribute(r, blocks[block], term * below[r] if kh == 2 and r < 2 else term, first, last)
+
+        def second():
+            for part, numbers in enumerate((upper, lower)):
+                yield from crossed_steps(
+                    units, 1, part, numbers, w_ref, 0, block, depth, rows, flat_row)
+            yield 0, lambda: crossed_pops(units, [(1, upper), (1, lower)], rows, give)
+            yield from taps(1, first_tile, [0], {0: 0, 4: 1})
+
+        merged(
+            [taps(0, first_tile, [3, 1, 2], {r: r for r in range(ACCS)}), second()],
+            lambda: queue.some(RATE))
         inner = pltpu.make_async_copy(
             inner_s, out_hbm.at[final, pl.ds(1, rows - 2)], i_sem)
         inner.start()
@@ -412,6 +543,7 @@
         inner.wait()
         for copy in copies:
             copy.wait()
+        late.wait()
 
     pl.run_scoped(run, *[pltpu.ACC(m)((width, SIDE), F32) for m in range(MXUS) for _ in range(ACCS)])
 
@@ -446,7 +578,7 @@
     weight = inside(weight)
     near = swap(near, 0)
     far = swap(far, 1)
-    out, part, last, carry, nacc = pl.pallas_call(
+    out, part, last, carry, nacc, late = pl.pallas_call(
         interior,
         out_shape=(
             jax.ShapeDtypeStruct(latents.shape, BF16),
@@ -454,16 +586,17 @@
             pltpu.VMEM((rows, width, deep), BF16),
             pltpu.VMEM((rows, width, chans), F32),
             pltpu.VMEM((frames, width, chans), F32),
+            pltpu.VMEM((rows - 2, width, chans), BF16),
         ),
         in_specs=[smem, smem, vmem, vmem, vmem, vmem, vmem],
-        out_specs=(anywhere,) + (vmem,) * 4,
+        out_specs=(anywhere,) + (vmem,) * 5,
         scratch_shapes=[
-            pltpu.VMEM((rows + 1, width + 16, chans), F32),
+            pltpu.VMEM((rows + 1, chans // LANES, width + 16, LANES), F32),
             pltpu.VMEM((frames - 1, rows, width, deep), BF16),
             pltpu.VMEM((frames, width, deep), BF16),
-            pltpu.VMEM((frames, rows, width, chans), F32),
-            pltpu.VMEM((frames - 1, rows - 2, width, chans), BF16),
-            dma((frames - 1,)),
+            pltpu.VMEM((frames - 1, rows, width, chans), F32),
+            pltpu.VMEM((frames - 2, rows - 2, width, chans), BF16),
+            dma((frames - 2,)),
         ],
         cost_estimate=pl.CostEstimate(
             flops=2 * 84 * width * deep * chans, bytes_accessed=14 * 2**20, transcendentals=0
@@ -474,11 +607,11 @@
     return pl.pallas_call(
         edges,
         out_shape=jax.ShapeDtypeStruct(latents.shape, BF16),
-        in_specs=[smem, smem] + [vmem] * 7 + [anywhere],
+        in_specs=[smem, smem] + [vmem] * 8 + [anywhere],
         out_specs=anywhere,
-        input_output_aliases={9: 0},
+        input_output_aliases={10: 0},
         scratch_shapes=[
-            pltpu.VMEM((1, width + 16, chans), F32),
+            pltpu.VMEM((1, chans // LANES, width + 16, LANES), F32),
             pltpu.VMEM((frames, width, deep), BF16),
             pltpu.VMEM((rows, width, chans), F32),
             pltpu.VMEM((frames, width, chans), F32),
@@ -486,6 +619,7 @@
             pltpu.VMEM((frames, 2, width, chans), BF16),
             pltpu.VMEM((rows - 2, width, chans), BF16),
             dma((frames, 2)),
+            dma(()),
             dma(()),
         ],
         cost_estimate=pl.CostEstimate(
@@ -495,7 +629,7 @@
         name="edges",
     )(
         intersection, ramp, inside(far), weight, gamma, inside(part), inside(last),
-        inside(carry), inside(nacc), out,
+        inside(carry), inside(nacc), inside(late), out,
     )
 
 

time: 29 us -> 27.7 us (0.955)
  Pallas kernels: 23.7 us -> 22.3 us
    pallas_call x1, Pallas kernels: 17 us -> 16 us  [per_device(): pl.pallas_call(interior, out_shape=(jax.ShapeDtypeStruct(latents.shape, B...]
    pallas_call x1, Pallas kernels: 5.28 us -> 4.95 us  [per_device(): pl.pallas_call(edges, out_shape=jax.ShapeDtypeStruct(latents.shape, BF16)...]
  transfers between devices with their start and end apart: 2 -> 2, of which waited for: 0 -> 0; matrix products, arithmetic and copies ran while one was open for 0% -> 0% of each run, Pallas kernels for 59% -> 58%
where the time goes in v4:
time: 27.7 us; the launch traced here: 27.5 us
  Pallas kernels  22.3 us (81%)
  starting transfers between devices  4.88 us (18%)
  between operations  0.29 us (1%)
    pallas_call x1, Pallas kernels, per_device(): pl.pallas_call(interior, out_shape=(jax.ShapeDtypeStruct(latents.shape, B...  16 us
    pallas_call x1, Pallas kernels, per_device(): pl.pallas_call(edges, out_shape=jax.ShapeDtypeStruct(latents.shape, BF16)...  4.95 us
    ppermute x2, starting transfers between devices, per_device(): lax.ppermute(array, 'rows', [pair for k in range(start, count - 1, 2) for...  4.88 us
    pallas_call x1, Pallas kernels, per_device(): pl.pallas_call(select, out_shape=(halo, halo), in_specs=[hbm], out_specs=...  1.36 us
  transfers between devices with their start and end apart: 2, of which 0 were waited for; matrix products, arithmetic and copies ran while one was open for 0% of the time, Pallas kernels for 58%

profile of v4, /device:TPU:1, one launch (start us, length us, event | category | flops | bytes accessed | tf_op | source)
XLA Modules:
  0.0 27.5 jit_solution(5983990030918043255)
XLA Ops:
  0.0 0.0 copy-start.3
  0.0 0.0 copy-start.4
  0.0 0.0 copy-start.5
  0.0 0.0 copy-start.2
  0.0 0.0 copy-start.1
  0.0 0.0 copy-start
  0.0 1.4 %select.1 = (bf16[4,160,384]{2,1,0:T(8,128)(2,1)S(1)}, bf16[4,160,384]{2,1,0:T(8,128)(2,1)S(1)}) custom-call(bf16[4,4,160,384]{3,2,1,0:T(8,128)(2,1)} %x_ref.1), custom_call_target="tpu_custom_call" | custom-call | flops 20000000000 | bytes 4194304 | tf_op jit(solution)/shard_map/select/pallas_call | solution.py:568
  1.4 0.1 collective-permute-start.1
  1.5 4.8 %collective-permute-start = (bf16[4,160,384]{2,1,0:T(8,128)(2,1)S(1)}, bf16[4,160,384]{2,1,0:T(8,128)(2,1)S(1)}, u32[]{:S(2)}, u32[]{:S(2)}) collective-permute-start(bf16[4,160,384]{2,1,0:T(8,128)(2,1)S(1)} %get-tuple-element.13), channel_id=1, source_target_pairs={{1,2},{2,1},{3,4},{4,3},{5,6},{6,5},{7,8},{8,7},{9,10},{10,9},{11,... | collective-permute-start | bytes 1474568 | tf_op jit(solution)/shard_map/ppermute | solution.py:565
  6.3 0.0 copy-done.4
  6.3 0.0 copy-done.5
  6.3 0.0 collective-permute-done.1.near_ref
  6.3 0.0 copy-done.3
  6.4 0.0 copy-done.2
  6.4 0.0 copy-done.1
  6.4 0.0 copy-done
  6.4 16.0 %interior.1 = (bf16[4,4,160,384]{3,2,1,0:T(8,128)(2,1)}, f32[3,2,160,384]{3,2,1,0:T(8,128)S(1)}, bf16[4,160,1152]{2,1,0:T(8,128)(2,1)S(1)}, f32[4,160,384]{2,1,0...) custom-call(s32[16]{0:T(128)S(1)} %copy-done.1, s32[16]{0:T(128)S(1)} %copy-done.2, ...), custom_call_target="tpu_custom_call" | custom-call | flops 11890851840 | bytes 14680064 | tf_op jit(solution)/shard_map/interior/pallas_call | solution.py:581
  22.4 0.0 collective-permute-done.far_ref
  22.4 5.0 %edges.1 = bf16[4,4,160,384]{3,2,1,0:T(8,128)(2,1)} custom-call(s32[16]{0:T(128)S(1)} %copy-done.1, s32[16]{0:T(128)S(1)} %copy-done.2, bf16[4,160,384]{2,1,0:T(8,128)(2,1)S(1)} %collective-permute-done.far_ref, bf16[3,3,1152,384]{3,2,1,0:T(8,128)(2,1)S(1)} %bitcast.2, f32[1,384]{1,0:T(1,128)S(1)} %reshape.10.gamma_ref, ...), custom_call_target="tpu_custom_call", output_to_operand_aliasing={{}: (10, {})} | custom-call | flops 3397386240 | bytes 4194304 | tf_op jit(solution)/shard_map/edges/pallas_call | solution.py:607
  (2 shorter events, 0.0 us)
Async XLA Ops:
  0.0 6.3 %copy-start.3 = (bf16[4,4,160,384]{3,2,1,0:T(8,128)(2,1)S(1)}, bf16[4,4,160,384]{3,2,1,0:T(8,128)(2,1)}, u32[]{:S(2)}) copy-start(bf16[4,4,160,384]{3,2,1,0:T(8,128)(2,1)} %x_ref.1) | copy-start | bytes 5898244
  0.0 6.3 %copy-start.4 = (f32[384]{0:T(512)S(1)}, f32[384]{0:T(512)}, u32[]{:S(2)}) copy-start(f32[384]{0:T(512)} %param.7) | copy-start | bytes 4612
  0.0 6.3 %copy-start.5 = (f32[384]{0:T(512)S(1)}, f32[384]{0:T(512)}, u32[]{:S(2)}) copy-start(f32[384]{0:T(512)} %param.9) | copy-start | bytes 4612
  0.0 6.3 %copy-start.2 = (s32[16]{0:T(128)S(1)}, s32[16]{0:T(128)}, u32[]{:S(2)}) copy-start(s32[16]{0:T(128)} %ramp_ref.3) | copy-start | bytes 196
  0.0 6.3 %copy-start.1 = (s32[16]{0:T(128)S(1)}, s32[16]{0:T(128)}, u32[]{:S(2)}) copy-start(s32[16]{0:T(128)} %inter_ref.3) | copy-start | bytes 196
  0.0 6.3 %copy-start = (bf16[3,3,3,384,384]{4,3,2,1,0:T(8,128)(2,1)S(1)}, bf16[3,3,3,384,384]{4,3,2,1,0:T(8,128)(2,1)}, u32[]{:S(2)}) copy-start(bf16[3,3,3,384,384]{4,3,2,1,0:T(8,128)(2,1)} %param.8) | copy-start | bytes 23887876
  1.4 4.9 %collective-permute-start.1 = (bf16[4,160,384]{2,1,0:T(8,128)(2,1)S(1)}, bf16[4,160,384]{2,1,0:T(8,128)(2,1)S(1)}, u32[]{:S(2)}, u32[]{:S(2)}) collective-permute-start(bf16[4,160,384]{2,1,0:T(8,128)(2,1)S(1)} %get-tuple-element.14), channel_id=1, source_target_pairs={{0,1},{1,0},{2,3},{3,2},{4,5},{5,4},{6,7},{7,6},{8,9},{9,8},{10,11... | collective-permute-start | bytes 1474568 | tf_op jit(solution)/shard_map/ppermute | solution.py:565
  1.5 20.9 %collective-permute-start = (bf16[4,160,384]{2,1,0:T(8,128)(2,1)S(1)}, bf16[4,160,384]{2,1,0:T(8,128)(2,1)S(1)}, u32[]{:S(2)}, u32[]{:S(2)}) collective-permute-start(bf16[4,160,384]{2,1,0:T(8,128)(2,1)S(1)} %get-tuple-element.13), channel_id=1, source_target_pairs={{1,2},{2,1},{3,4},{4,3},{5,6},{6,5},{7,8},{8,7},{9,10},{10,9},{11,... | collective-permute-start | bytes 1474568 | tf_op jit(solution)/shard_map/ppermute | solution.py:565

commit v5 on v4

--- a/solution.py
+++ b/solution.py
@@ -10,7 +10,7 @@
 TAPS = 3
 LANES = 128
 SIDE = 256
-RATE = 0.3
+RATE = 0.4
 CHUNK = 80
 MXUS = 2
 ACCS = 6
@@ -175,7 +175,7 @@
     return beside(parts)
 
 
-def matrix_job(units, job, passes, rows, flat_row, weight, step, pop, between=None):
+def matrix_job(units, job, passes, rows, flat_row, weight, step, pop):
     for number, places in enumerate(passes):
         active = [
             (m, tile, [r for r in rows_of if acc_of(r, places, rows) is not None])
@@ -191,8 +191,6 @@
                     if r in rows_of:
                         units.add(m, acc_of(r, places, rows), block)
                 step()
-        if between is not None and number == len(passes) - 3:
-            between()
         for r in (3, 1, 0, 2):
             here = acc_of(r, places, rows)
             later = [acc_of(r, other, rows) for other in passes[number + 1 :]]
@@ -252,6 +250,66 @@
             term = product[:, half * LANES : (half + 1) * LANES]
             give(r, kh, term, r not in order[:seen], r not in order[seen + 1 :])
             seen += 1
+
+
+def halo_jobs(frames, depth):
+    run = lambda f, slots: [(f, chunk, slots) for chunk in range(depth)]
+    wide = [
+        (sum((run(f, (g - f, g - f)) for f in range(max(0, g + 1 - TAPS), g + 1)), []), (0, 1), (g, g))
+        for g in range(frames)
+    ]
+    thin = [(run(f, (0, 1)), (2, 2), (f, f + 1)) for f in range(frames - 1)]
+    alone = {}
+    for f, slot in [(f, 2) for f in range(frames - 2)] + [(frames - 1, 0)]:
+        alone[f + slot] = alone.get(f + slot, []) + run(f, (slot,))
+    second = wide[:1] + thin
+    for g, entries in alone.items():
+        second.append((entries, (2,), (g,)))
+    second.sort(key=lambda job: (max(f for f, _, _ in job[0]), len(job[1]) < 2))
+    return wide[1:], second
+
+
+def halo_steps(units, m, jobs, w_ref, kh, flat_ref, give):
+    for number, (entries, blocks, made) in enumerate(jobs):
+        number = number % ACCS
+        for pair in in_pairs(entries):
+            def operand(pair=pair, blocks=blocks):
+                columns = []
+                for j, block in enumerate(blocks):
+                    parts = [
+                        w_ref[TAPS - 1 - slots[j], kh, chunk * LANES : (chunk + 1) * LANES,
+                              block * LANES : (block + 1) * LANES]
+                        for _, chunk, slots in pair
+                    ]
+                    while len(parts) < 2:
+                        parts.append(jnp.zeros((LANES, LANES), BF16))
+                    columns.append(jnp.concatenate(parts, axis=0))
+                while len(columns) < 2:
+                    columns.append(jnp.zeros((SIDE, LANES), BF16))
+                units.weights(m, jnp.concatenate(columns, axis=1))
+
+            def multiply(pair=pair, number=number):
+                units.add(m, number, beside([
+                    flat_ref[f, :, chunk * LANES : (chunk + 1) * LANES] for f, chunk, _ in pair]))
+
+            yield 0, operand
+            yield 1, multiply
+
+        def hand(number=number, blocks=blocks, made=made):
+            product = units.pop(m, number)
+            for j, (block, g) in enumerate(zip(blocks, made)):
+                give(g, block, product[:, j * LANES : (j + 1) * LANES])
+
+        yield 0, hand
+
+
+def halo_shares(frames, depth):
+    shares = {}
+    for jobs in halo_jobs(frames, depth):
+        for _, blocks, made in jobs:
+            for key in zip(made, blocks):
+                shares[key] = shares.get(key, 0) + 1
+    return shares
 
 
 def merged(streams, step):
@@ -341,32 +399,6 @@
                     f + slot, r, lanes, term,
                     (f == 0 or slot == 2) and number < 4, slot == 0 and last)
 
-        whole = [
-            (f, tile) for f in range(frames) for tile in tiles_of(chans, min(TAPS, frames - f))
-        ]
-        slots = in_pairs(whole)
-
-        def near(slot_pair, number=0):
-            for f, _ in slot_pair:
-                queue.until(ready[f])
-            for places in in_pairs([(near_kh, c) for c in range(depth)]):
-                low, high = places[0][1] * LANES, (places[-1][1] + 1) * LANES
-                for m, (f, tile) in enumerate(slot_pair):
-                    units.weights(m, cells(w_ref, tile, places))
-                for m, (f, tile) in enumerate(slot_pair):
-                    block = nflat[f, :, low:high]
-                    units.add(m, number, block if len(places) == 2 else beside([block]))
-
-        def near_pop(slot_pair, number=0):
-            for m, (f, tile) in enumerate(slot_pair):
-                product = units.pop(m, number)
-                for i, (slot, block) in enumerate(tile):
-                    lanes = slice(block * LANES, (block + 1) * LANES)
-                    term = product[:, i * LANES : (i + 1) * LANES]
-                    if f > 0 and slot < 2:
-                        term = term + nacc_ref[f + slot, :, lanes]
-                    nacc_ref[f + slot, :, lanes] = term
-
         queue.until(ready[0, 0])
         copies = []
         for f in range(frames - 1):
@@ -375,15 +407,12 @@
                 flat_row = lambda h: flat.at[f, h]
                 if f:
                     queue.until(ready[f, 0])
-                here = slots.pop(0)
                 matrix_job(
                     units, job, passes, rows, flat_row, weight,
-                    lambda: queue.some(RATE), lambda *rest: pop(f, *rest),
-                    lambda: near(here))
-                near_pop(here)
+                    lambda: queue.some(RATE), lambda *rest: pop(f, *rest))
             tile = tiles_of(chans, min(TAPS, frames - f))[-1]
             if len(tile) == 1:
-                (slot, block), here = tile[0], slots.pop(0)
+                (slot, block), = tile
                 numbers = {h: h for h in range(rows)}
                 flat_row = lambda h: flat.at[f, h]
                 merged([
@@ -391,7 +420,6 @@
                         units, part, part, numbers, w_ref, slot, block, depth, rows, flat_row)
                     for part in range(MXUS)
                 ], lambda: queue.some(RATE))
-                near(here, 4)
 
                 def give(r, kh, term, first, last):
                     if kh == 2 and r < 2:
@@ -401,14 +429,24 @@
                         first and (f == 0 or slot == 2), last and slot == 0)
 
                 crossed_pops(units, [(0, numbers), (1, numbers)], rows, give)
-                near_pop(here, 4)
             if f < frames - 2:
                 copies.append(pltpu.make_async_copy(
                     done_s.at[f], out_hbm.at[f, pl.ds(1, rows - 2)], o_sem.at[f]))
                 copies[-1].start()
-        for here in slots:
-            near(here)
-            near_pop(here)
+        queue.until(len(queue.items))
+        seen = set()
+
+        def near(g, block, term):
+            lanes = slice(block * LANES, (block + 1) * LANES)
+            if (g, block) in seen:
+                term = term + nacc_ref[g, :, lanes]
+            seen.add((g, block))
+            nacc_ref[g, :, lanes] = term
+
+        merged([
+            halo_steps(units, m, jobs, w_ref, near_kh, nflat, near)
+            for m, jobs in enumerate(halo_jobs(frames, depth))
+        ], lambda: None)
         for copy in copies:
             copy.wait()
 
@@ -506,40 +544,32 @@
         nears, copies = [], []
         for g in range(frames):
             nears.append(queue.add([lambda g=g, at=at: near_row(g, at) for at in range(0, width, CHUNK)]))
-        whole = [
-            (f, tile) for f in range(frames) for tile in tiles_of(chans, min(TAPS, frames - f))
-        ]
-        for number, pair in enumerate(in_pairs(whole)):
-            queue.until(ready[max(f for f, _ in pair)])
-            here = (number % 2) * 3
-            for places in in_pairs([(2 * odd, c) for c in range(depth)]):
-                low, high = places[0][1] * LANES, (places[-1][1] + 1) * LANES
-                for m, (f, tile) in enumerate(pair):
-                    units.weights(m, cells(w_ref, tile, places))
-                for m, (f, tile) in enumerate(pair):
-                    block = fflat[f, :, low:high]
-                    units.add(m, here, block if len(places) == 2 else beside([block]))
-                queue.some(1)
-            for m, (f, tile) in enumerate(pair):
-                product = units.pop(m, here)
-                for i, (slot, block) in enumerate(tile):
-                    g = f + slot
-                    lanes = blocks[block]
-                    term = product[:, i * LANES : (i + 1) * LANES]
-                    if f > 0 and slot < 2:
-                        term = term + facc[g, :, lanes]
-                    if slot > 0:
-                        facc[g, :, lanes] = term
-                        continue
-                    base = tail[odd, :, lanes] if g == final else part_ref[g, odd, :, lanes]
-                    done_s[g, odd, :, lanes] = (base + far_scale * term).astype(BF16)
-                    if block == len(blocks) - 1:
-                        queue.until(nears[g])
-                        for side in range(2):
-                            copies.append(pltpu.make_async_copy(
-                                done_s.at[g, side], out_hbm.at[g, side * (rows - 1)],
-                                o_sem.at[g, side]))
-                            copies[-1].start()
+        queue.until(ready[-1])
+        shares = halo_shares(frames, depth)
+        seen = {}
+
+        def give(g, block, term):
+            lanes = blocks[block]
+            seen[g, block] = seen.get((g, block), 0) + 1
+            if seen[g, block] > 1:
+                term = term + facc[g, :, lanes]
+            if seen[g, block] < shares[g, block]:
+                facc[g, :, lanes] = term
+                return
+            base = tail[odd, :, lanes] if g == final else part_ref[g, odd, :, lanes]
+            done_s[g, odd, :, lanes] = (base + far_scale * term).astype(BF16)
+            if all(seen.get((g, b)) == shares[g, b] for b in range(len(blocks))):
+                queue.until(nears[g])
+                for side in range(2):
+                    copies.append(pltpu.make_async_copy(
+                        done_s.at[g, side], out_hbm.at[g, side * (rows - 1)],
+                        o_sem.at[g, side]))
+                    copies[-1].start()
+
+        merged([
+            halo_steps(units, m, jobs, w_ref, 2 * odd, fflat, give)
+            for m, jobs in enumerate(halo_jobs(frames, depth))
+        ], lambda: queue.some(1))
         inner.wait()
         for copy in copies:
             copy.wait()

time: 27.7 us -> 27.5 us (level)
  no operation moved by 1% of the time
where the time goes in v5:
time: 27.5 us; the launch traced here: 27.3 us
  Pallas kernels  22.1 us (80%)
  starting transfers between devices  4.88 us (18%)
  between operations  0.29 us (1%)
    pallas_call x1, Pallas kernels, per_device(): pl.pallas_call(interior, out_shape=(jax.ShapeDtypeStruct(latents.shape, B...  15.8 us
    pallas_call x1, Pallas kernels, per_device(): pl.pallas_call(edges, out_shape=jax.ShapeDtypeStruct(latents.shape, BF16)...  4.95 us
    ppermute x2, starting transfers between devices, per_device(): lax.ppermute(array, 'rows', [pair for k in range(start, count - 1, 2) for...  4.88 us
    pallas_call x1, Pallas kernels, per_device(): pl.pallas_call(select, out_shape=(halo, halo), in_specs=[hbm], out_specs=...  1.36 us
  transfers between devices with their start and end apart: 2, of which 0 were waited for; matrix products, arithmetic and copies ran while one was open for 0% of the time, Pallas kernels for 58%

profile of v5, /device:TPU:1, one launch (start us, length us, event | category | flops | bytes accessed | tf_op | source)
XLA Modules:
  0.0 27.3 jit_solution(3128772743879635630)
XLA Ops:
  0.0 0.0 copy-start.3
  0.0 0.0 copy-start.4
  0.0 0.0 copy-start.5
  0.0 0.0 copy-start.2
  0.0 0.0 copy-start.1
  0.0 0.0 copy-start
  0.0 1.4 %select.1 = (bf16[4,160,384]{2,1,0:T(8,128)(2,1)S(1)}, bf16[4,160,384]{2,1,0:T(8,128)(2,1)S(1)}) custom-call(bf16[4,4,160,384]{3,2,1,0:T(8,128)(2,1)} %x_ref.1), custom_call_target="tpu_custom_call" | custom-call | flops 20000000000 | bytes 4194304 | tf_op jit(solution)/shard_map/select/pallas_call | solution.py:598
  1.4 0.1 collective-permute-start.1
  1.5 4.8 %collective-permute-start = (bf16[4,160,384]{2,1,0:T(8,128)(2,1)S(1)}, bf16[4,160,384]{2,1,0:T(8,128)(2,1)S(1)}, u32[]{:S(2)}, u32[]{:S(2)}) collective-permute-start(bf16[4,160,384]{2,1,0:T(8,128)(2,1)S(1)} %get-tuple-element.13), channel_id=1, source_target_pairs={{1,2},{2,1},{3,4},{4,3},{5,6},{6,5},{7,8},{8,7},{9,10},{10,9},{11,... | collective-permute-start | bytes 1474568 | tf_op jit(solution)/shard_map/ppermute | solution.py:595
  6.3 0.0 copy-done.4
  6.3 0.0 copy-done.5
  6.3 0.0 collective-permute-done.1.near_ref
  6.3 0.0 copy-done.3
  6.4 0.0 copy-done.2
  6.4 0.0 copy-done.1
  6.4 0.0 copy-done
  6.4 15.8 %interior.1 = (bf16[4,4,160,384]{3,2,1,0:T(8,128)(2,1)}, f32[3,2,160,384]{3,2,1,0:T(8,128)S(1)}, bf16[4,160,1152]{2,1,0:T(8,128)(2,1)S(1)}, f32[4,160,384]{2,1,0...) custom-call(s32[16]{0:T(128)S(1)} %copy-done.1, s32[16]{0:T(128)S(1)} %copy-done.2, ...), custom_call_target="tpu_custom_call" | custom-call | flops 11890851840 | bytes 14680064 | tf_op jit(solution)/shard_map/interior/pallas_call | solution.py:611
  22.2 0.0 collective-permute-done.far_ref
  22.2 5.0 %edges.1 = bf16[4,4,160,384]{3,2,1,0:T(8,128)(2,1)} custom-call(s32[16]{0:T(128)S(1)} %copy-done.1, s32[16]{0:T(128)S(1)} %copy-done.2, bf16[4,160,384]{2,1,0:T(8,128)(2,1)S(1)} %collective-permute-done.far_ref, bf16[3,3,1152,384]{3,2,1,0:T(8,128)(2,1)S(1)} %bitcast.2, f32[1,384]{1,0:T(1,128)S(1)} %reshape.10.gamma_ref, ...), custom_call_target="tpu_custom_call", output_to_operand_aliasing={{}: (10, {})} | custom-call | flops 3397386240 | bytes 4194304 | tf_op jit(solution)/shard_map/edges/pallas_call | solution.py:637
  (2 shorter events, 0.0 us)
Async XLA Ops:
  0.0 6.3 %copy-start.3 = (bf16[4,4,160,384]{3,2,1,0:T(8,128)(2,1)S(1)}, bf16[4,4,160,384]{3,2,1,0:T(8,128)(2,1)}, u32[]{:S(2)}) copy-start(bf16[4,4,160,384]{3,2,1,0:T(8,128)(2,1)} %x_ref.1) | copy-start | bytes 5898244
  0.0 6.3 %copy-start.4 = (f32[384]{0:T(512)S(1)}, f32[384]{0:T(512)}, u32[]{:S(2)}) copy-start(f32[384]{0:T(512)} %param.7) | copy-start | bytes 4612
  0.0 6.3 %copy-start.5 = (f32[384]{0:T(512)S(1)}, f32[384]{0:T(512)}, u32[]{:S(2)}) copy-start(f32[384]{0:T(512)} %param.9) | copy-start | bytes 4612
  0.0 6.3 %copy-start.2 = (s32[16]{0:T(128)S(1)}, s32[16]{0:T(128)}, u32[]{:S(2)}) copy-start(s32[16]{0:T(128)} %ramp_ref.3) | copy-start | bytes 196
  0.0 6.3 %copy-start.1 = (s32[16]{0:T(128)S(1)}, s32[16]{0:T(128)}, u32[]{:S(2)}) copy-start(s32[16]{0:T(128)} %inter_ref.3) | copy-start | bytes 196
  0.0 6.3 %copy-start = (bf16[3,3,3,384,384]{4,3,2,1,0:T(8,128)(2,1)S(1)}, bf16[3,3,3,384,384]{4,3,2,1,0:T(8,128)(2,1)}, u32[]{:S(2)}) copy-start(bf16[3,3,3,384,384]{4,3,2,1,0:T(8,128)(2,1)} %param.8) | copy-start | bytes 23887876
  1.4 4.9 %collective-permute-start.1 = (bf16[4,160,384]{2,1,0:T(8,128)(2,1)S(1)}, bf16[4,160,384]{2,1,0:T(8,128)(2,1)S(1)}, u32[]{:S(2)}, u32[]{:S(2)}) collective-permute-start(bf16[4,160,384]{2,1,0:T(8,128)(2,1)S(1)} %get-tuple-element.14), channel_id=1, source_target_pairs={{0,1},{1,0},{2,3},{3,2},{4,5},{5,4},{6,7},{7,6},{8,9},{9,8},{10,11... | collective-permute-start | bytes 1474568 | tf_op jit(solution)/shard_map/ppermute | solution.py:595
  1.5 20.7 %collective-permute-start = (bf16[4,160,384]{2,1,0:T(8,128)(2,1)S(1)}, bf16[4,160,384]{2,1,0:T(8,128)(2,1)S(1)}, u32[]{:S(2)}, u32[]{:S(2)}) collective-permute-start(bf16[4,160,384]{2,1,0:T(8,128)(2,1)S(1)} %get-tuple-element.13), channel_id=1, source_target_pairs={{1,2},{2,1},{3,4},{4,3},{5,6},{6,5},{7,8},{8,7},{9,10},{10,9},{11,... | collective-permute-start | bytes 1474568 | tf_op jit(solution)/shard_map/ppermute | solution.py:595

commit v6 on v5

--- a/solution.py
+++ b/solution.py
@@ -1,3 +1,5 @@
+import itertools
+
 import jax
 import jax.numpy as jnp
 from jax import lax
@@ -497,6 +499,10 @@
                 tail[0 if r == 0 else 1, :, lanes] = term
             else:
                 inner_s[r - 1, :, lanes] = term.astype(BF16)
+            if last:
+                made.append(r)
+                if len(made) == rows * len(blocks):
+                    settle()
 
         def pop(m, tile, number, r, kept, last):
             product = units.pop(m, number)
@@ -535,20 +541,26 @@
             yield 0, lambda: crossed_pops(units, [(1, upper), (1, lower)], rows, give)
             yield from taps(1, first_tile, [0], {0: 0, 4: 1})
 
-        merged(
-            [taps(0, first_tile, [3, 1, 2], {r: r for r in range(ACCS)}), second()],
-            lambda: queue.some(RATE))
+        copies, made = [], []
         inner = pltpu.make_async_copy(
             inner_s, out_hbm.at[final, pl.ds(1, rows - 2)], i_sem)
-        inner.start()
-        nears, copies = [], []
-        for g in range(frames):
-            nears.append(queue.add([lambda g=g, at=at: near_row(g, at) for at in range(0, width, CHUNK)]))
-        queue.until(ready[-1])
+
+        def send(g, kind):
+            side = (1 - odd, odd)[kind]
+            copies.append(pltpu.make_async_copy(
+                done_s.at[g, side], out_hbm.at[g, side * (rows - 1)], o_sem.at[g, kind]))
+            copies[-1].start()
+
+        def settle():
+            inner.start()
+            for g in range(frames):
+                queue.add([lambda g=g, at=at: near_row(g, at) for at in range(0, width, CHUNK)])
+                queue.add([lambda g=g: send(g, 0)])
+
         shares = halo_shares(frames, depth)
         seen = {}
 
-        def give(g, block, term):
+        def collect(g, block, term):
             lanes = blocks[block]
             seen[g, block] = seen.get((g, block), 0) + 1
             if seen[g, block] > 1:
@@ -559,17 +571,18 @@
             base = tail[odd, :, lanes] if g == final else part_ref[g, odd, :, lanes]
             done_s[g, odd, :, lanes] = (base + far_scale * term).astype(BF16)
             if all(seen.get((g, b)) == shares[g, b] for b in range(len(blocks))):
-                queue.until(nears[g])
-                for side in range(2):
-                    copies.append(pltpu.make_async_copy(
-                        done_s.at[g, side], out_hbm.at[g, side * (rows - 1)],
-                        o_sem.at[g, side]))
-                    copies[-1].start()
+                send(g, 1)
+
+        def halo(m):
+            yield 0, lambda: queue.until(ready[-1])
+            yield from halo_steps(
+                units, m, halo_jobs(frames, depth)[m], w_ref, 2 * odd, fflat, collect)
 
         merged([
-            halo_steps(units, m, jobs, w_ref, 2 * odd, fflat, give)
-            for m, jobs in enumerate(halo_jobs(frames, depth))
-        ], lambda: queue.some(1))
+            itertools.chain(taps(0, first_tile, [3, 1, 2], {r: r for r in range(ACCS)}), halo(0)),
+            itertools.chain(second(), halo(1)),
+        ], lambda: queue.some(RATE))
+        queue.until(len(queue.items))
         inner.wait()
         for copy in copies:
             copy.wait()

time: 27.5 us -> 27.4 us (level)
  no operation moved by 1% of the time
where the time goes in v6:
time: 27.4 us; the launch traced here: 27.3 us
  Pallas kernels  22.1 us (81%)
  starting transfers between devices  4.88 us (18%)
  between operations  0.29 us (1%)
    pallas_call x1, Pallas kernels, per_device(): pl.pallas_call(interior, out_shape=(jax.ShapeDtypeStruct(latents.shape, B...  15.8 us
    pallas_call x1, Pallas kernels, per_device(): pl.pallas_call(edges, out_shape=jax.ShapeDtypeStruct(latents.shape, BF16)...  4.92 us
    ppermute x2, starting transfers between devices, per_device(): lax.ppermute(array, 'rows', [pair for k in range(start, count - 1, 2) for...  4.88 us
    pallas_call x1, Pallas kernels, per_device(): pl.pallas_call(select, out_shape=(halo, halo), in_specs=[hbm], out_specs=...  1.36 us
  transfers between devices with their start and end apart: 2, of which 0 were waited for; matrix products, arithmetic and copies ran while one was open for 0% of the time, Pallas kernels for 58%

profile of v6, /device:TPU:1, one launch (start us, length us, event | category | flops | bytes accessed | tf_op | source)
XLA Modules:
  0.0 27.3 jit_solution(14016519803152068074)
XLA Ops:
  0.0 0.0 copy-start.3
  0.0 0.0 copy-start.4
  0.0 0.0 copy-start.5
  0.0 0.0 copy-start.2
  0.0 0.0 copy-start.1
  0.0 0.0 copy-start
  0.0 1.4 %select.1 = (bf16[4,160,384]{2,1,0:T(8,128)(2,1)S(1)}, bf16[4,160,384]{2,1,0:T(8,128)(2,1)S(1)}) custom-call(bf16[4,4,160,384]{3,2,1,0:T(8,128)(2,1)} %x_ref.1), custom_call_target="tpu_custom_call" | custom-call | flops 20000000000 | bytes 4194304 | tf_op jit(solution)/shard_map/select/pallas_call | solution.py:611
  1.4 0.1 collective-permute-start.1
  1.5 4.8 %collective-permute-start = (bf16[4,160,384]{2,1,0:T(8,128)(2,1)S(1)}, bf16[4,160,384]{2,1,0:T(8,128)(2,1)S(1)}, u32[]{:S(2)}, u32[]{:S(2)}) collective-permute-start(bf16[4,160,384]{2,1,0:T(8,128)(2,1)S(1)} %get-tuple-element.13), channel_id=1, source_target_pairs={{1,2},{2,1},{3,4},{4,3},{5,6},{6,5},{7,8},{8,7},{9,10},{10,9},{11,... | collective-permute-start | bytes 1474568 | tf_op jit(solution)/shard_map/ppermute | solution.py:608
  6.3 0.0 copy-done.4
  6.3 0.0 copy-done.5
  6.3 0.0 collective-permute-done.1.near_ref
  6.3 0.0 copy-done.3
  6.4 0.0 copy-done.2
  6.4 0.0 copy-done.1
  6.4 0.0 copy-done
  6.4 15.8 %interior.1 = (bf16[4,4,160,384]{3,2,1,0:T(8,128)(2,1)}, f32[3,2,160,384]{3,2,1,0:T(8,128)S(1)}, bf16[4,160,1152]{2,1,0:T(8,128)(2,1)S(1)}, f32[4,160,384]{2,1,0...) custom-call(s32[16]{0:T(128)S(1)} %copy-done.1, s32[16]{0:T(128)S(1)} %copy-done.2, ...), custom_call_target="tpu_custom_call" | custom-call | flops 11890851840 | bytes 14680064 | tf_op jit(solution)/shard_map/interior/pallas_call | solution.py:624
  22.2 0.0 collective-permute-done.far_ref
  22.2 4.9 %edges.1 = bf16[4,4,160,384]{3,2,1,0:T(8,128)(2,1)} custom-call(s32[16]{0:T(128)S(1)} %copy-done.1, s32[16]{0:T(128)S(1)} %copy-done.2, bf16[4,160,384]{2,1,0:T(8,128)(2,1)S(1)} %collective-permute-done.far_ref, bf16[3,3,1152,384]{3,2,1,0:T(8,128)(2,1)S(1)} %bitcast.2, f32[1,384]{1,0:T(1,128)S(1)} %reshape.10.gamma_ref, ...), custom_call_target="tpu_custom_call", output_to_operand_aliasing={{}: (10, {})} | custom-call | flops 3397386240 | bytes 4194304 | tf_op jit(solution)/shard_map/edges/pallas_call | solution.py:650
  (2 shorter events, 0.0 us)
Async XLA Ops:
  0.0 6.3 %copy-start.3 = (bf16[4,4,160,384]{3,2,1,0:T(8,128)(2,1)S(1)}, bf16[4,4,160,384]{3,2,1,0:T(8,128)(2,1)}, u32[]{:S(2)}) copy-start(bf16[4,4,160,384]{3,2,1,0:T(8,128)(2,1)} %x_ref.1) | copy-start | bytes 5898244
  0.0 6.3 %copy-start.4 = (f32[384]{0:T(512)S(1)}, f32[384]{0:T(512)}, u32[]{:S(2)}) copy-start(f32[384]{0:T(512)} %param.7) | copy-start | bytes 4612
  0.0 6.3 %copy-start.5 = (f32[384]{0:T(512)S(1)}, f32[384]{0:T(512)}, u32[]{:S(2)}) copy-start(f32[384]{0:T(512)} %param.9) | copy-start | bytes 4612
  0.0 6.3 %copy-start.2 = (s32[16]{0:T(128)S(1)}, s32[16]{0:T(128)}, u32[]{:S(2)}) copy-start(s32[16]{0:T(128)} %ramp_ref.3) | copy-start | bytes 196
  0.0 6.3 %copy-start.1 = (s32[16]{0:T(128)S(1)}, s32[16]{0:T(128)}, u32[]{:S(2)}) copy-start(s32[16]{0:T(128)} %inter_ref.3) | copy-start | bytes 196
  0.0 6.3 %copy-start = (bf16[3,3,3,384,384]{4,3,2,1,0:T(8,128)(2,1)S(1)}, bf16[3,3,3,384,384]{4,3,2,1,0:T(8,128)(2,1)}, u32[]{:S(2)}) copy-start(bf16[3,3,3,384,384]{4,3,2,1,0:T(8,128)(2,1)} %param.8) | copy-start | bytes 23887876
  1.4 4.9 %collective-permute-start.1 = (bf16[4,160,384]{2,1,0:T(8,128)(2,1)S(1)}, bf16[4,160,384]{2,1,0:T(8,128)(2,1)S(1)}, u32[]{:S(2)}, u32[]{:S(2)}) collective-permute-start(bf16[4,160,384]{2,1,0:T(8,128)(2,1)S(1)} %get-tuple-element.14), channel_id=1, source_target_pairs={{0,1},{1,0},{2,3},{3,2},{4,5},{5,4},{6,7},{7,6},{8,9},{9,8},{10,11... | collective-permute-start | bytes 1474568 | tf_op jit(solution)/shard_map/ppermute | solution.py:608
  1.5 20.7 %collective-permute-start = (bf16[4,160,384]{2,1,0:T(8,128)(2,1)S(1)}, bf16[4,160,384]{2,1,0:T(8,128)(2,1)S(1)}, u32[]{:S(2)}, u32[]{:S(2)}) collective-permute-start(bf16[4,160,384]{2,1,0:T(8,128)(2,1)S(1)} %get-tuple-element.13), channel_id=1, source_target_pairs={{1,2},{2,1},{3,4},{4,3},{5,6},{6,5},{7,8},{8,7},{9,10},{10,9},{11,... | collective-permute-start | bytes 1474568 | tf_op jit(solution)/shard_map/ppermute | solution.py:608

commit v7 on v6

--- a/solution.py
+++ b/solution.py
@@ -12,8 +12,9 @@
 TAPS = 3
 LANES = 128
 SIDE = 256
-RATE = 0.4
-CHUNK = 80
+RATE = 1.8
+ORDER = (3, 1, 2, 0)
+CHUNK = 16
 MXUS = 2
 ACCS = 6
 
@@ -139,16 +140,16 @@
     def __init__(self, accs):
         self.accs = [accs[m * ACCS : (m + 1) * ACCS] for m in range(MXUS)]
         self.stage = [0] * MXUS
-        self.load = [None] * MXUS
+        self.waiting = [[] for _ in range(MXUS)]
 
     def weights(self, m, operand):
         pltpu.matmul_push_rhs(operand, self.stage[m], m)
-        self.load[m] = self.stage[m]
+        self.waiting[m].append(self.stage[m])
         self.stage[m] = 1 - self.stage[m]
 
-    def add(self, m, number, block):
-        pltpu.matmul_acc_lhs(self.accs[m][number], block, self.load[m])
-        self.load[m] = None
+    def add(self, m, number, block, fresh):
+        load = self.waiting[m].pop(0) if fresh else None
+        pltpu.matmul_acc_lhs(self.accs[m][number], block, load)
 
     def pop(self, m, number):
         return pltpu.matmul_pop(self.accs[m][number])
@@ -178,20 +179,28 @@
 
 
 def matrix_job(units, job, passes, rows, flat_row, weight, step, pop):
-    for number, places in enumerate(passes):
-        active = [
-            (m, tile, [r for r in rows_of if acc_of(r, places, rows) is not None])
+    def active(places):
+        return [
+            (m, tile, [r for r in ORDER if r in rows_of and acc_of(r, places, rows) is not None])
             for m, (tile, rows_of) in enumerate(job)
         ]
-        for m, tile, rows_of in active:
+
+    def push(places):
+        for m, tile, rows_of in active(places):
             if rows_of:
                 units.weights(m, weight(tile, places))
-        for r in (3, 1, 2, 0):
-            if any(r in rows_of for _, _, rows_of in active):
+
+    push(passes[0])
+    for number, places in enumerate(passes):
+        if number + 1 < len(passes):
+            push(passes[number + 1])
+        here = active(places)
+        for r in ORDER:
+            if any(r in rows_of for _, _, rows_of in here):
                 block = row_block(flat_row, r, places)
-                for m, _, rows_of in active:
+                for m, _, rows_of in here:
                     if r in rows_of:
-                        units.add(m, acc_of(r, places, rows), block)
+                        units.add(m, acc_of(r, places, rows), block, r == rows_of[0])
                 step()
         for r in (3, 1, 0, 2):
             here = acc_of(r, places, rows)
@@ -236,7 +245,7 @@
             m, crossed(w_ref, slot, block, khs, chunks))
         for h in heights:
             yield 1, lambda chunks=chunks, h=h: units.add(m, numbers[h], beside(
-                [flat_row(h)[:, c * LANES : (c + 1) * LANES] for c in chunks]))
+                [flat_row(h)[:, c * LANES : (c + 1) * LANES] for c in chunks]), h == heights[0])
 
 
 def crossed_pops(units, places, rows, give):
@@ -292,7 +301,7 @@
 
             def multiply(pair=pair, number=number):
                 units.add(m, number, beside([
-                    flat_ref[f, :, chunk * LANES : (chunk + 1) * LANES] for f, chunk, _ in pair]))
+                    flat_ref[f, :, chunk * LANES : (chunk + 1) * LANES] for f, chunk, _ in pair]), True)
 
             yield 0, operand
             yield 1, multiply
@@ -516,8 +525,8 @@
                 if active:
                     yield 0, lambda places=places: units.weights(m, cells(w_ref, tile, places))
                 for r in active:
-                    yield 1, lambda r=r, places=places: units.add(
-                        m, numbers[acc_of(r, places, rows)], row_block(flat_row, r, places))
+                    yield 1, lambda r=r, places=places, active=active: units.add(
+                        m, numbers[acc_of(r, places, rows)], row_block(flat_row, r, places), r == active[0])
                 for r in active:
                     here = acc_of(r, places, rows)
                     later = [acc_of(r, other, rows) for other in passes[number + 1 :]]

time: 27.4 us -> 27.4 us (level)
  transfers between devices with their start and end apart: 2 -> 2, of which waited for: 0 -> 0; matrix products, arithmetic and copies ran while one was open for 0% -> 0% of each run, Pallas kernels for 58% -> 57%
where the time goes in v7:
time: 27.4 us; the launch traced here: 27.3 us
  Pallas kernels  22 us (80%)
  starting transfers between devices  4.88 us (18%)
  between operations  0.29 us (1%)
    pallas_call x1, Pallas kernels, per_device(): pl.pallas_call(interior, out_shape=(jax.ShapeDtypeStruct(latents.shape, B...  15.6 us
    pallas_call x1, Pallas kernels, per_device(): pl.pallas_call(edges, out_shape=jax.ShapeDtypeStruct(latents.shape, BF16)...  5.08 us
    ppermute x2, starting transfers between devices, per_device(): lax.ppermute(array, 'rows', [pair for k in range(start, count - 1, 2) for...  4.88 us
    pallas_call x1, Pallas kernels, per_device(): pl.pallas_call(select, out_shape=(halo, halo), in_specs=[hbm], out_specs=...  1.36 us
  transfers between devices with their start and end apart: 2, of which 0 were waited for; matrix products, arithmetic and copies ran while one was open for 0% of the time, Pallas kernels for 57%

profile of v7, /device:TPU:1, one launch (start us, length us, event | category | flops | bytes accessed | tf_op | source)
XLA Modules:
  0.0 27.3 jit_solution(4857115439869553999)
XLA Ops:
  0.0 0.0 copy-start.3
  0.0 0.0 copy-start.4
  0.0 0.0 copy-start.5
  0.0 0.0 copy-start.2
  0.0 0.0 copy-start.1
  0.0 0.0 copy-start
  0.0 1.4 %select.1 = (bf16[4,160,384]{2,1,0:T(8,128)(2,1)S(1)}, bf16[4,160,384]{2,1,0:T(8,128)(2,1)S(1)}) custom-call(bf16[4,4,160,384]{3,2,1,0:T(8,128)(2,1)} %x_ref.1), custom_call_target="tpu_custom_call" | custom-call | flops 20000000000 | bytes 4194304 | tf_op jit(solution)/shard_map/select/pallas_call | solution.py:620
  1.4 0.1 collective-permute-start.1
  1.5 4.8 %collective-permute-start = (bf16[4,160,384]{2,1,0:T(8,128)(2,1)S(1)}, bf16[4,160,384]{2,1,0:T(8,128)(2,1)S(1)}, u32[]{:S(2)}, u32[]{:S(2)}) collective-permute-start(bf16[4,160,384]{2,1,0:T(8,128)(2,1)S(1)} %get-tuple-element.13), channel_id=1, source_target_pairs={{1,2},{2,1},{3,4},{4,3},{5,6},{6,5},{7,8},{8,7},{9,10},{10,9},{11,... | collective-permute-start | bytes 1474568 | tf_op jit(solution)/shard_map/ppermute | solution.py:617
  6.3 0.0 copy-done.4
  6.3 0.0 copy-done.5
  6.3 0.0 collective-permute-done.1.near_ref
  6.3 0.0 copy-done.3
  6.4 0.0 copy-done.2
  6.4 0.0 copy-done.1
  6.4 0.0 copy-done
  6.4 15.6 %interior.1 = (bf16[4,4,160,384]{3,2,1,0:T(8,128)(2,1)}, f32[3,2,160,384]{3,2,1,0:T(8,128)S(1)}, bf16[4,160,1152]{2,1,0:T(8,128)(2,1)S(1)}, f32[4,160,384]{2,1,0...) custom-call(s32[16]{0:T(128)S(1)} %copy-done.1, s32[16]{0:T(128)S(1)} %copy-done.2, ...), custom_call_target="tpu_custom_call" | custom-call | flops 11890851840 | bytes 14680064 | tf_op jit(solution)/shard_map/interior/pallas_call | solution.py:633
  22.0 0.0 collective-permute-done.far_ref
  22.0 5.1 %edges.1 = bf16[4,4,160,384]{3,2,1,0:T(8,128)(2,1)} custom-call(s32[16]{0:T(128)S(1)} %copy-done.1, s32[16]{0:T(128)S(1)} %copy-done.2, bf16[4,160,384]{2,1,0:T(8,128)(2,1)S(1)} %collective-permute-done.far_ref, bf16[3,3,1152,384]{3,2,1,0:T(8,128)(2,1)S(1)} %bitcast.2, f32[1,384]{1,0:T(1,128)S(1)} %reshape.10.gamma_ref, ...), custom_call_target="tpu_custom_call", output_to_operand_aliasing={{}: (10, {})} | custom-call | flops 3397386240 | bytes 4194304 | tf_op jit(solution)/shard_map/edges/pallas_call | solution.py:659
  (2 shorter events, 0.0 us)
Async XLA Ops:
  0.0 6.3 %copy-start.3 = (bf16[4,4,160,384]{3,2,1,0:T(8,128)(2,1)S(1)}, bf16[4,4,160,384]{3,2,1,0:T(8,128)(2,1)}, u32[]{:S(2)}) copy-start(bf16[4,4,160,384]{3,2,1,0:T(8,128)(2,1)} %x_ref.1) | copy-start | bytes 5898244
  0.0 6.3 %copy-start.4 = (f32[384]{0:T(512)S(1)}, f32[384]{0:T(512)}, u32[]{:S(2)}) copy-start(f32[384]{0:T(512)} %param.7) | copy-start | bytes 4612
  0.0 6.3 %copy-start.5 = (f32[384]{0:T(512)S(1)}, f32[384]{0:T(512)}, u32[]{:S(2)}) copy-start(f32[384]{0:T(512)} %param.9) | copy-start | bytes 4612
  0.0 6.3 %copy-start.2 = (s32[16]{0:T(128)S(1)}, s32[16]{0:T(128)}, u32[]{:S(2)}) copy-start(s32[16]{0:T(128)} %ramp_ref.3) | copy-start | bytes 196
  0.0 6.3 %copy-start.1 = (s32[16]{0:T(128)S(1)}, s32[16]{0:T(128)}, u32[]{:S(2)}) copy-start(s32[16]{0:T(128)} %inter_ref.3) | copy-start | bytes 196
  0.0 6.3 %copy-start = (bf16[3,3,3,384,384]{4,3,2,1,0:T(8,128)(2,1)S(1)}, bf16[3,3,3,384,384]{4,3,2,1,0:T(8,128)(2,1)}, u32[]{:S(2)}) copy-start(bf16[3,3,3,384,384]{4,3,2,1,0:T(8,128)(2,1)} %param.8) | copy-start | bytes 23887876
  1.4 4.9 %collective-permute-start.1 = (bf16[4,160,384]{2,1,0:T(8,128)(2,1)S(1)}, bf16[4,160,384]{2,1,0:T(8,128)(2,1)S(1)}, u32[]{:S(2)}, u32[]{:S(2)}) collective-permute-start(bf16[4,160,384]{2,1,0:T(8,128)(2,1)S(1)} %get-tuple-element.14), channel_id=1, source_target_pairs={{0,1},{1,0},{2,3},{3,2},{4,5},{5,4},{6,7},{7,6},{8,9},{9,8},{10,11... | collective-permute-start | bytes 1474568 | tf_op jit(solution)/shard_map/ppermute | solution.py:617
  1.5 20.5 %collective-permute-start = (bf16[4,160,384]{2,1,0:T(8,128)(2,1)S(1)}, bf16[4,160,384]{2,1,0:T(8,128)(2,1)S(1)}, u32[]{:S(2)}, u32[]{:S(2)}) collective-permute-start(bf16[4,160,384]{2,1,0:T(8,128)(2,1)S(1)} %get-tuple-element.13), channel_id=1, source_target_pairs={{1,2},{2,1},{3,4},{4,3},{5,6},{6,5},{7,8},{8,7},{9,10},{10,9},{11,... | collective-permute-start | bytes 1474568 | tf_op jit(solution)/shard_map/ppermute | solution.py:617
